TPU v7x, 32 devices: a whole 2x2x4 slice. The times are simulated.
32 devices in a mesh: groups: 2 (over x), ctx: 16 (over z, y, core).
Axes of the slice: x: 2, y: 2, z: 4, core: 2. Of those that a mesh axis runs over, the one named last changes fastest.
Arguments:
- queries: bfloat16 [256, 2048], P(('groups', 'ctx')), parts along dimension 0, may hold values from -8 to 8, as said below
- keys: bfloat16 [2, 8192, 256], P('groups', 'ctx'), parts along dimension 0, may hold values from -8 to 8
- values: bfloat16 [2, 8192, 256], P('groups', 'ctx'), parts along dimension 0, may hold values from -16 to 16
- lengths: int32 [2], P('groups'), parts along dimension 0, may hold values from 4096 to 8192, as said below
- owner_counts: int32 [32], P('groups'), parts along dimension 0, may hold values from 1 to 16, 128 in all
- row_order: int32 [256], P('groups'), parts along dimension 0, may hold values from 0 to 127, each once
- residual: bfloat16 [512, 2048], P(('groups', 'ctx')), parts along dimension 0, may hold values from -40 to 40, as said below
- out_weight: bfloat16 [2048, 2048], P('ctx'), may hold values from -0.125 to 0.125
- norm_gain: float32 [2048], replicated, may hold values from 0.1 to 1.9
- expert_ids: int32 [512, 8], P(('groups', 'ctx')), parts along dimension 0, may hold values from 0 to 15, all different within a row; in each aligned block of 16 rows (0 to 15, 16 to 31, ...) at most 16 rows name the same one
- route_weights: float32 [512, 8], P(('groups', 'ctx')), parts along dimension 0, may hold values from 0.1 to 1
- gate_up: bfloat16 [16, 2048, 1536], P('ctx'), may hold values from -0.125 to 0.125
- expert_down: bfloat16 [16, 768, 2048], P('ctx'), may hold values from -0.21875 to 0.21875
Outputs:
- attn_slots: bfloat16 [512, 2048], P(('groups', 'ctx')), parts along dimension 0
- layer_out: bfloat16 [512, 2048], P(('groups', 'ctx')), parts along dimension 0
There are 2 independent parts, one for each index of `groups`. A program takes and returns all parts, laid end to end along the dimension named above; an argument that names none is the same for every part. Nothing has to cross between parts.
Inputs may be any that keep to these rules, and one draw needn't show every extreme that they name: Large entries of queries and keys may line up. `lengths`: at least 4096; one request has exactly 8192. `owner_counts`: sum to 128; the largest is exactly 16. `row_order`: each row once. `residual`: entries may be any real values in the range. `expert_ids`: each slot names 8 different experts; within the 16 slots of one owner no expert is named more than 16 times, and some expert exactly that many times.
All inputs are finite; a program needn't handle non-finite values.
Results may differ from a plain program's by a relative error of at most 0.009.
Values may be sent and summed in bfloat16 or wider, within the bound.
A program may use at most 128 MiB of HBM per device.

v0:
```python
import jax
import jax.numpy as jnp
from jax import lax
from jax.sharding import PartitionSpec as P

D = 2048
HQ = 16
KVH = 2
HD = 128
EFF = 768
TOPK = 8
STRETCH = 128


def slot_table(owner_counts, row_order, total_rows, capacity):
    offsets = jnp.cumsum(owner_counts) - owner_counts
    column = jnp.arange(capacity, dtype=jnp.int32)
    where_at = offsets[:, None] + column[None, :]
    filled = column[None, :] < owner_counts[:, None]
    picked = row_order[jnp.clip(where_at, 0, total_rows - 1)]
    return jnp.where(filled, picked, total_rows)


def partial_attention(query_rows, key_block, value_block, lengths, first_key):
    requests = lengths.shape[0]
    groups = HQ // KVH
    span = key_block.shape[1]
    query_grid = query_rows.reshape(requests, STRETCH, KVH, groups, HD)
    key_grid = key_block.reshape(requests, span, KVH, HD)
    value_grid = value_block.reshape(requests, span, KVH, HD)

    def one_request(items):
        query_part, key_part, value_part, length = items
        scores = jnp.einsum(
            "cvgh,pvh->vgcp", query_part, key_part, preferred_element_type=jnp.float32
        ) * HD ** (-0.5)
        query_pos = length - STRETCH + jnp.arange(STRETCH, dtype=jnp.int32)
        key_pos = first_key + jnp.arange(span, dtype=jnp.int32)
        allowed = key_pos[None, :] <= query_pos[:, None]
        scores = jnp.where(allowed, scores, -1e30)
        top = jnp.max(scores, axis=-1)
        weights = jnp.where(allowed, jnp.exp(scores - top[..., None]), 0.0)
        total = jnp.sum(weights, axis=-1)
        mixed = jnp.einsum(
            "vgcp,pvh->cvgh",
            weights.astype(jnp.bfloat16),
            value_part,
            preferred_element_type=jnp.float32,
        )
        return (
            mixed.reshape(STRETCH, HQ * HD),
            jnp.transpose(top, (2, 0, 1)).reshape(STRETCH, HQ),
            jnp.transpose(total, (2, 0, 1)).reshape(STRETCH, HQ),
        )

    mixed, top, total = lax.map(one_request, (query_grid, key_grid, value_grid, lengths))
    return (mixed.reshape(-1, HQ * HD), top.reshape(-1, HQ), total.reshape(-1, HQ))


def merge_sources(parts):
    mixed, top, total = parts
    sources = mixed.shape[0]
    items = mixed.shape[1]
    best = jnp.max(top, axis=0)
    factor = jnp.exp(top - best[None])
    denom = jnp.sum(factor * total, axis=0)
    numer = jnp.sum(mixed.reshape(sources, items, HQ, HD) * factor[..., None], axis=0)
    return (numer / denom[..., None]).reshape(items, HQ * HD).astype(jnp.bfloat16)


def body(
    queries,
    keys,
    values,
    lengths,
    owner_counts,
    row_order,
    residual,
    out_weight,
    norm_gain,
    expert_ids,
    route_weights,
    gate_up,
    expert_down,
):
    device = lax.axis_index("ctx")
    width = lax.axis_size("ctx")
    local_len = keys.shape[1]
    every_query = lax.all_gather(queries, "ctx", axis=0, tiled=True)
    mixed, top, total = partial_attention(every_query, keys, values, lengths, device * local_len)
    row_count = every_query.shape[0]
    capacity = residual.shape[0]
    slot_rows = slot_table(owner_counts, row_order, row_count, capacity)
    home_count = row_count // width
    mixed_home = mixed.reshape(width, home_count, HQ * HD)
    top_home = top.reshape(width, home_count, HQ)
    total_home = total.reshape(width, home_count, HQ)
    home_rows = merge_sources(
        (
            lax.all_to_all(mixed_home, "ctx", split_axis=0, concat_axis=0, tiled=True),
            lax.all_to_all(top_home, "ctx", split_axis=0, concat_axis=0, tiled=True),
            lax.all_to_all(total_home, "ctx", split_axis=0, concat_axis=0, tiled=True),
        )
    )
    all_rows = lax.all_gather(home_rows, "ctx", axis=0, tiled=True)
    all_rows = jnp.concatenate([all_rows, jnp.zeros((1, HQ * HD), jnp.bfloat16)], axis=0)
    attn_own = all_rows[slot_rows[device]]
    own_valid = jnp.arange(capacity, dtype=jnp.int32) < owner_counts[device]
    projected = jnp.dot(
        attn_own,
        lax.all_gather(out_weight, "ctx", axis=0, tiled=True),
        preferred_element_type=jnp.float32,
    )
    stream = (residual.astype(jnp.float32) + projected).astype(jnp.bfloat16)
    stream_f = stream.astype(jnp.float32)
    normed = (
        stream_f
        * lax.rsqrt(jnp.mean(stream_f * stream_f, axis=-1, keepdims=True) + 1e-06)
        * norm_gain
    ).astype(jnp.bfloat16)
    route_cap = min(capacity, max(2, 2 * capacity * TOPK // width))
    flat_ids = expert_ids.reshape(-1)
    hits = (flat_ids[:, None] == jnp.arange(width, dtype=jnp.int32)[None, :]).astype(jnp.int32)
    before = jnp.cumsum(hits, axis=0) - hits
    ranks = jnp.sum(before * hits, axis=1)
    target = (flat_ids * route_cap + ranks).reshape(capacity, TOPK)
    weight_norm = route_weights / jnp.sum(route_weights, axis=-1, keepdims=True)
    slot_index = jnp.arange(width * route_cap, dtype=jnp.int32)
    match = (target[None, :, :] == slot_index[:, None, None]) & own_valid[None, :, None]
    dispatch = jnp.any(match, axis=-1).astype(jnp.bfloat16)
    outgoing = (
        jnp.dot(dispatch, normed, preferred_element_type=jnp.float32)
        .astype(jnp.bfloat16)
        .reshape(width, route_cap, D)
    )
    arrived = lax.all_to_all(outgoing, "ctx", split_axis=0, concat_axis=0, tiled=True)
    rows = arrived.reshape(-1, D)
    both = jnp.dot(rows, gate_up[0], preferred_element_type=jnp.float32)
    hidden = (jax.nn.silu(both[:, :EFF]) * both[:, EFF:]).astype(jnp.bfloat16)
    result = jnp.dot(hidden, expert_down[0], preferred_element_type=jnp.float32).astype(
        jnp.bfloat16
    )
    returned = lax.all_to_all(
        result.reshape(arrived.shape), "ctx", split_axis=0, concat_axis=0, tiled=True
    )
    combine = jnp.transpose(jnp.sum(match.astype(jnp.float32) * weight_norm[None], axis=-1))
    moe = jnp.dot(
        combine, returned.reshape(-1, D).astype(jnp.float32), precision=lax.Precision.HIGHEST
    )
    layer_out = jnp.where(own_valid[:, None], stream_f + moe, 0.0).astype(jnp.bfloat16)
    return (attn_own, layer_out)


def solution(mesh):
    placed = (
        P(("groups", "ctx"), None),
        P("groups", "ctx", None),
        P("groups", "ctx", None),
        P("groups"),
        P("groups"),
        P("groups"),
        P(("groups", "ctx"), None),
        P("ctx", None),
        P(),
        P(("groups", "ctx"), None),
        P(("groups", "ctx"), None),
        P("ctx", None, None),
        P("ctx", None, None),
    )
    return jax.shard_map(
        body,
        mesh=mesh,
        in_specs=placed,
        out_specs=(P(("groups", "ctx"), None), P(("groups", "ctx"), None)),
        check_vma=False,
    )
```

profile of v0, /device:TPU:0, one launch (start us, length us, event | category | flops | bytes accessed | tf_op | source)
XLA Modules:
  0.0 211.7 jit_solution(12911379524427185722)
XLA Ops:
  7.2 0.7 all-gather.2.cloned.1.call-update
  8.8 27.6 %all_gather.9 = bf16[128,2048]{1,0:T(8,128)(2,1)} all-gather(bf16[8,2048]{1,0:T(8,128)(2,1)} %param.13), channel_id=1, replica_groups=mesh['groups'=2,'ctx'=16] {'ctx'}, dimensions={0}, use_global_device_ids=true | all-gather | bytes 557056 | tf_op jit(solution)/shard_map/all_gather | solution.py:89
  36.4 2.1 %copy.61 = bf16[128,2048]{0,1:T(8,128)(2,1)} copy(bf16[128,2048]{1,0:T(8,128)(2,1)} %all_gather.9) | data formatting | bytes 1048576 | tf_op jit(solution)/shard_map/all_gather | solution.py:89
  38.5 1.0 squeeze.29
  39.7 1.8 fusion.2
  41.5 2.0 copy-done.2
  43.5 1.0 fusion.5
  44.7 0.7 reshape.208
  45.4 3.5 %all-to-all-start.2 = ((f32[16,1,128]{2,1,0:T(1,128)}), f32[16,1,128]{2,1,0:T(1,128)S(1)}, u32[]{:S(2)}, u32[]{:S(2)}) async-start(f32[16,1,128]{2,1,0:T(1,128)} %reshape.208), calls=%async_computation.2 | async-start | bytes 16384 | tf_op jit(solution)/shard_map/all_to_all | solution.py:102
  49.2 0.7 reshape.206
  49.8 1.0 squeeze.31
  50.9 4.5 %all-to-all-done.2 = f32[16,1,128]{2,1,0:T(1,128)S(1)} async-done(((f32[16,1,128]{2,1,0:T(1,128)}), f32[16,1,128]{2,1,0:T(1,128)S(1)}, u32[]{:S(2)}, u32[]{:S(2)}) %all-to-all-start.2) | async-done | bytes 8224 | tf_op jit(solution)/shard_map/all_to_all | solution.py:102
  55.4 3.5 %all-to-all-start.1 = ((f32[16,1,128]{2,1,0:T(1,128)}), f32[16,1,128]{2,1,0:T(1,128)S(1)}, u32[]{:S(2)}, u32[]{:S(2)}) async-start(f32[16,1,128]{2,1,0:T(1,128)} %reshape.206), calls=%async_computation.1 | async-start | bytes 16384 | tf_op jit(solution)/shard_map/all_to_all | solution.py:101
  58.8 3.6 %fusion.17 = f32[128,2,8,128]{3,0,2,1:T(8,128)S(1)} fusion(f32[2,512,128,8]{2,1,3,0:T(8,128)} %copy-done.2, f32[2,8,128]{2,1,0:T(8,128)S(1)} %get-tuple-element.22, pred[128,512]{0,1:T(8,128)(4,1)S(1)} %broadcast_compare_fusion, bf16[512,2,128,1]{2,1,0,3:T(2,128)(2,1)S(1)} %bitcast.71), kind=kOutput, calls=%fused_computation.21 | convolution fusion | flops 273678336 | bytes 5578752 | tf_op jit(solution)/shard_map/while/body/eval_jaxpr/vgcp,pvh->cvgh/dot_general | solution.py:44
  62.4 1.6 copy.66
  64.0 2.5 %reshape_reshape.9 = f32[16,8,2048]{2,1,0:T(8,128)} reshape(f32[128,2,8,128]{3,2,1,0:T(8,128)} %copy.66) | data formatting | bytes 2097152 | tf_op jit(solution)/shard_map/reshape;reshape | solution.py:95
  66.5 6.0 %all-to-all-start = ((f32[16,8,2048]{2,1,0:T(8,128)}), f32[16,8,2048]{2,1,0:T(8,128)}, u32[]{:S(2)}, u32[]{:S(2)}) async-start(f32[16,8,2048]{2,1,0:T(8,128)} %reshape_reshape.9), calls=%async_computation | async-start | bytes 2097152 | tf_op jit(solution)/shard_map/all_to_all | solution.py:100
  73.6 1.9 gather_fusion
  76.2 0.7 fusion.34
  79.0 0.7 reduce.3
  80.0 25.6 %all-to-all-done = f32[16,8,2048]{2,1,0:T(8,128)} async-done(((f32[16,8,2048]{2,1,0:T(8,128)}), f32[16,8,2048]{2,1,0:T(8,128)}, u32[]{:S(2)}, u32[]{:S(2)}) %all-to-all-start) | async-done | bytes 1048608 | tf_op jit(solution)/shard_map/all_to_all | solution.py:100
  105.6 1.6 fusion.20
  107.3 25.1 %all_gather.10 = bf16[128,2048]{1,0:T(8,128)(2,1)S(1)} all-gather(bf16[8,2048]{1,0:T(8,128)(2,1)S(1)} %fusion.29), channel_id=1, replica_groups=mesh['groups'=2,'ctx'=16] {'ctx'}, dimensions={0}, use_global_device_ids=true | all-gather | bytes 557056 | tf_op jit(solution)/shard_map/all_gather | solution.py:105
  132.4 0.9 concatenate.3
  133.3 1.8 gather_fusion.1
  135.1 4.7 %multiply_reduce_fusion = (f32[16]{0:T(128)S(1)}, f32[16,2048]{1,0:T(8,128)S(1)}) fusion(bf16[16,2048]{1,0:T(8,128)(2,1)S(1)} %gather_fusion.1, bf16[2048,2048]{1,0:T(8,128)(2,1)} %all-gather.2.cloned.1.call-done, bf16[16,2048]{1,0:T(8,128)(2,1)S(1)} %copy-done.4), kind=kOutput, calls=%fused_computation.31 | convolution fusion | flops 134414320 | bytes 8650816 | tf_op jit(solution)/shard_map/dot_general | solution.py:109
  140.4 27.4 %all_to_all.25 = bf16[16,16,2048]{2,1,0:T(8,128)(2,1)S(1)} all-to-all(bf16[16,16,2048]{2,1,0:T(8,128)(2,1)S(1)} %bitcast.66), channel_id=1, replica_groups=mesh['groups'=2,'ctx'=16] {'ctx'}, dimensions={0} | all-to-all | bytes 2097152 | tf_op jit(solution)/shard_map/all_to_all | solution.py:136
  167.8 4.6 %fusion = f32[256,1536]{1,0:T(8,128)S(1)} fusion(bf16[256,2048]{1,0:T(8,128)(2,1)S(1)} %bitcast.70, bf16[1,2048,1536]{2,1,0:T(8,128)(2,1)} %param.24), kind=kOutput, calls=%fused_computation.2 | convolution fusion | flops 1610612736 | bytes 8912896 | tf_op jit(solution)/shard_map/dot_general | solution.py:138
  172.4 2.1 fusion.7
  174.5 5.0 %all-to-all-start.4 = ((bf16[16,16,2048]{2,1,0:T(8,128)(2,1)}), bf16[16,16,2048]{2,1,0:T(8,128)(2,1)}, u32[]{:S(2)}, u32[]{:S(2)}) async-start(bf16[16,16,2048]{2,1,0:T(8,128)(2,1)} %bitcast.69), calls=%async_computation.4 | async-start | bytes 2097152 | tf_op jit(solution)/shard_map/all_to_all | solution.py:143
  179.7 22.7 %all-to-all-done.4 = bf16[16,16,2048]{2,1,0:T(8,128)(2,1)} async-done(((bf16[16,16,2048]{2,1,0:T(8,128)(2,1)}), bf16[16,16,2048]{2,1,0:T(8,128)(2,1)}, u32[]{:S(2)}, u32[]{:S(2)}) %all-to-all-start.4) | async-done | bytes 1048608 | tf_op jit(solution)/shard_map/all_to_all | solution.py:143
  202.4 2.4 %fusion.11 = bf16[16,2048]{1,0:T(8,128)(2,1)} fusion(f32[16,2048]{1,0:T(8,128)S(1)} %get-tuple-element.25, f32[256,16]{0,1:T(8,128)S(1)} %select_reduce_fusion, bf16[256,2048]{1,0:T(8,128)(2,1)} %bitcast.19, pred[16]{0:T(512)(128)(4,1)S(1)} %iota_compare_fusion.2), kind=kOutput, calls=%fused_computation.16 | convolution fusion | flops 100761600 | bytes 1261584 | tf_op jit(solution)/shard_map/dot_general | solution.py:147
  (61 shorter events, 5.6 us)
Async XLA Ops:
  7.2 165.2 %copy-start = (bf16[1,768,2048]{2,1,0:T(8,128)(2,1)S(1)}, bf16[1,768,2048]{2,1,0:T(8,128)(2,1)}, u32[]{:S(2)}) copy-start(bf16[1,768,2048]{2,1,0:T(8,128)(2,1)} %param.25) | copy-start | bytes 9437188
  7.2 127.9 %all-gather.2.cloned.1.call-start = ((), (), s32[]{:S(2)}) async-start(), calls=%async_computation.5 | async-start | bytes 8912896 | tf_op jit(solution)/shard_map/all_gather | solution.py:111
  41.5 2.0 copy-start.2
  45.4 9.9 %all-to-all-start.2 = ((f32[16,1,128]{2,1,0:T(1,128)}), f32[16,1,128]{2,1,0:T(1,128)S(1)}, u32[]{:S(2)}, u32[]{:S(2)}) async-start(f32[16,1,128]{2,1,0:T(1,128)} %reshape.208), calls=%async_computation.2 | async-start | bytes 16384 | tf_op jit(solution)/shard_map/all_to_all | solution.py:102
  55.4 11.1 %all-to-all-start.1 = ((f32[16,1,128]{2,1,0:T(1,128)}), f32[16,1,128]{2,1,0:T(1,128)S(1)}, u32[]{:S(2)}, u32[]{:S(2)}) async-start(f32[16,1,128]{2,1,0:T(1,128)} %reshape.206), calls=%async_computation.1 | async-start | bytes 16384 | tf_op jit(solution)/shard_map/all_to_all | solution.py:101
  62.4 10.1 %copy-start.8 = (s32[16]{0:T(128)S(1)}, s32[16]{0:T(128)}, u32[]{:S(2)}) copy-start(s32[16]{0:T(128)} %param.17) | copy-start | bytes 196
  62.4 11.1 %copy-start.1 = (s32[128]{0:T(128)S(1)}, s32[128]{0:T(128)}, u32[]{:S(2)}) copy-start(s32[128]{0:T(128)} %param.18) | copy-start | bytes 1540
  66.5 39.1 %all-to-all-start = ((f32[16,8,2048]{2,1,0:T(8,128)}), f32[16,8,2048]{2,1,0:T(8,128)}, u32[]{:S(2)}, u32[]{:S(2)}) async-start(f32[16,8,2048]{2,1,0:T(8,128)} %reshape_reshape.9), calls=%async_computation | async-start | bytes 2097152 | tf_op jit(solution)/shard_map/all_to_all | solution.py:100
  73.5 2.0 copy-start.7
  75.4 59.7 %copy-start.4 = (bf16[16,2048]{1,0:T(8,128)(2,1)S(1)}, bf16[16,2048]{1,0:T(8,128)(2,1)}, u32[]{:S(2)}) copy-start(bf16[16,2048]{1,0:T(8,128)(2,1)} %param.19) | copy-start | bytes 196612
  135.1 4.8 %copy-start.3 = (bf16[16,2048]{1,0:T(8,128)(2,1)}, bf16[16,2048]{1,0:T(8,128)(2,1)S(1)}, u32[]{:S(2)}) copy-start(bf16[16,2048]{1,0:T(8,128)(2,1)S(1)} %gather_fusion.1) | copy-start | bytes 196612
  135.1 4.8 %copy-start.6 = (f32[2048]{0:T(1024)S(1)}, f32[2048]{0:T(1024)}, u32[]{:S(2)}) copy-start(f32[2048]{0:T(1024)} %param.21) | copy-start | bytes 24580
  172.4 7.1 %copy-start.5 = (f32[16,8]{0,1:T(8,128)S(1)}, f32[16,8]{0,1:T(8,128)}, u32[]{:S(2)}) copy-start(f32[16,8]{0,1:T(8,128)} %param.23) | copy-start | bytes 1540
  174.5 28.0 %all-to-all-start.4 = ((bf16[16,16,2048]{2,1,0:T(8,128)(2,1)}), bf16[16,16,2048]{2,1,0:T(8,128)(2,1)}, u32[]{:S(2)}, u32[]{:S(2)}) async-start(bf16[16,16,2048]{2,1,0:T(8,128)(2,1)} %bitcast.69), calls=%async_computation.4 | async-start | bytes 2097152 | tf_op jit(solution)/shard_map/all_to_all | solution.py:143
Sparse Core Ops, SparseCore 0:
  10.2 95.9 all-gather.1
where the time goes:
time: 214 us; the launch traced here: 212 us
  blocking collectives  80.2 us (37%)
  waiting for transfers between devices  53.6 us (25%)
  matrix products  19.6 us (9%)
  local copies, waits for them, and re-layouts  18.6 us (9%)
  starting transfers between devices  18 us (8%)
  between operations  15.3 us (7%)
  other arithmetic  6.55 us (3%)
    all_gather x1, blocking collectives, body(): every_query = lax.all_gather(queries, 'ctx', axis=0, tiled=True)  27.6 us
    all_to_all x1, blocking collectives, body(): lax.all_to_all(outgoing, 'ctx', split_axis=0, concat_axis=0, tiled=True)  27.4 us
    all_to_all x1, waiting for transfers between devices, body(): lax.all_to_all(mixed_home, 'ctx', split_axis=0, concat_axis=0, tiled=True)  25.6 us
    all_gather x1, blocking collectives, body(): all_rows = lax.all_gather(home_rows, 'ctx', axis=0, tiled=True)  25.1 us
    all_to_all x1, waiting for transfers between devices, body(): lax.all_to_all(result.reshape(arrived.shape), 'ctx', split_axis=0, concat...  22.7 us
    all_to_all x1, starting transfers between devices, body(): lax.all_to_all(mixed_home, 'ctx', split_axis=0, concat_axis=0, tiled=True)  6.02 us
    all_to_all x1, starting transfers between devices, body(): lax.all_to_all(result.reshape(arrived.shape), 'ctx', split_axis=0, concat...  4.97 us
    dot_general x1, matrix products, body(): jnp.dot(attn_own, lax.all_gather(out_weight, 'ctx', axis=0, tiled=True),...  4.69 us
  transfers between devices with their start and end apart: 5, of which 3 were waited for; matrix products, arithmetic and copies ran while one was open for 13% of the time, Pallas kernels for 0%

commit v1 on v0

v1 whole, which is shorter than its diff:
```python
import functools

import jax
import jax.numpy as jnp
from jax import lax
from jax.experimental import pallas as pl
from jax.experimental.pallas import tpu as pltpu
from jax.sharding import PartitionSpec as P

D = 2048
HQ = 16
KVH = 2
HD = 128
EFF = 768
TOPK = 8
STRETCH = 128
GROUPS = HQ // KVH
LANES = 128
F32 = jnp.float32
BF16 = jnp.bfloat16
MESH = pl.DeviceIdType.MESH


def dot(a, b, ca, cb):
    return lax.dot_general(a, b, (((ca,), (cb,)), ((), ())), preferred_element_type=F32)


def kernel(
    n,
    lengths,
    counts_ref,
    order_ref,
    q_ref,
    keys_ref,
    values_ref,
    residual_ref,
    ids_ref,
    route_ref,
    gain_ref,
    ow_hbm,
    gu_hbm,
    down_hbm,
    attn_out,
    layer_out,
    ow,
    gu,
    down,
    q_all,
    c_all,
    mix_snd,
    st_snd,
    mix_rcv,
    st_rcv,
    m_snd,
    s_snd,
    m_in,
    s_in,
    a_snd,
    a_in,
    p_snd,
    p_rcv,
    p_mid,
    p_in,
    n_all,
    hid,
    e_snd,
    e_rcv,
    e_mid,
    e_in,
    w_sem,
    q_s,
    q_f,
    q_r,
    c_s,
    c_f,
    c_r,
    pair_s,
    pair_r,
    m_s,
    m_r,
    s_s,
    s_r,
    a_s,
    a_r,
    p_s,
    p_r,
    n_s,
    n_f,
    n_r,
    e_s,
    e_r,
):
    half_n = n // 2
    home = q_ref.shape[0]
    rows = n * home
    cap = residual_ref.shape[0]
    slots = n * cap
    chunk = ow.shape[0]
    span = keys_ref.shape[1]
    requests = keys_ref.shape[0]
    me = lax.axis_index("ctx")
    par = lax.rem(me, 2)
    half = me // 2
    other = 1 - par
    sib = half * 2 + other

    def peer(k):
        return lax.rem(half + k, half_n)

    def remote(src, dst, ss, rs, dev):
        return pltpu.make_async_remote_copy(
            src_ref=src, dst_ref=dst, send_sem=ss, recv_sem=rs,
            device_id={"ctx": dev}, device_id_type=MESH,
        )

    def each(lo, hi, f):
        def step(k, c):
            f(k)
            return c
        lax.fori_loop(lo, hi, step, 0)

    loads = [
        pltpu.make_async_copy(ow_hbm, ow, w_sem.at[0]),
        pltpu.make_async_copy(gu_hbm.at[0], gu, w_sem.at[1]),
        pltpu.make_async_copy(down_hbm.at[0], down, w_sem.at[2]),
    ]

    barrier = pltpu.get_barrier_semaphore()
    each(1, n, lambda k: pl.semaphore_signal(
        barrier, inc=1, device_id={"ctx": lax.rem(me + k, n)}, device_id_type=MESH))

    qf = q_ref[...].astype(F32)
    width = GROUPS * HD
    q_all[par, half] = jnp.concatenate(
        [qf[:, v * width:(v + 1) * width] for v in range(KVH)], axis=0).astype(BF16)

    counts = counts_ref[...].astype(F32)

    def slot_info(index, owner, place):
        lane = lax.broadcasted_iota(jnp.int32, (index, n), 1)
        start = jnp.sum(jnp.where(lane < owner, counts, 0.0), axis=1, keepdims=True)
        held = jnp.sum(jnp.where(lane == owner, counts, 0.0), axis=1, keepdims=True)
        return start, place.astype(F32) < held

    own_place = lax.broadcasted_iota(jnp.int32, (cap, 1), 0)
    _, own_valid = slot_info(cap, jnp.zeros((cap, 1), jnp.int32) + me, own_place)

    ids = ids_ref[...]
    route = route_ref[...]
    route = route / jnp.sum(route, axis=1, keepdims=True)
    expert_lane = lax.broadcasted_iota(jnp.int32, (cap, c_all.shape[-1]), 1)
    mixw = jnp.zeros((cap, c_all.shape[-1]), F32)
    for k in range(TOPK):
        mixw = mixw + jnp.where(expert_lane == ids[:, k:k + 1], route[:, k:k + 1], 0.0)
    c_all[par, half] = jnp.where(own_valid, mixw, 0.0)

    pl.semaphore_wait(barrier, n - 1)

    def gather_start(buf, ss, rs):
        own = buf.at[par, half]
        each(1, half_n, lambda k: remote(
            own, own, ss.at[k], rs.at[par, half], peer(k) * 2 + par).start())
        remote(own, own, ss.at[0], rs.at[par, half], sib).start()

    def gather_forward(buf, ss, fs, rs):
        def step(k):
            q = lax.rem(half - k + half_n, half_n)
            block = buf.at[par, q]
            got = remote(block, block, ss.at[k], rs.at[par, q], sib)
            got.wait_recv()
            remote(block, block, fs.at[k], rs.at[par, q], sib).start()
        each(1, half_n, step)

    def gather_finish(buf, ss, fs, rs):
        def step(q):
            block = buf.at[other, q]
            remote(block, block, ss.at[0], rs.at[other, q], sib).wait_recv()
        each(0, half_n, step)
        own = buf.at[par, half]
        each(0, half_n, lambda k: remote(
            own, own, ss.at[k], rs.at[par, half], sib).wait_send())
        each(1, half_n, lambda k: remote(
            own, own, fs.at[k], rs.at[par, half], sib).wait_send())

    gather_start(q_all, q_s, q_r)
    gather_start(c_all, c_s, c_r)
    for load in loads:
        load.start()

    index = lax.broadcasted_iota(jnp.int32, (slots, 1), 0)
    block_of = index // cap
    owner = lax.rem(block_of, half_n) * 2 + block_of // half_n
    place = lax.rem(index, cap)
    start, filled = slot_info(slots, owner, place)
    at = start + place.astype(F32)
    row_lane = lax.broadcasted_iota(jnp.int32, (slots, rows), 1).astype(F32)
    order = order_ref[...].astype(F32)
    row_of = jnp.sum(jnp.where(row_lane == at, order, 0.0), axis=1, keepdims=True)
    row_of = jnp.where(filled, row_of, -1.0)
    pick = (row_lane == row_of).astype(BF16)

    gather_forward(q_all, q_s, q_f, q_r)
    gather_finish(q_all, q_s, q_f, q_r)

    first_key = me * span
    per_head = HD // chunk
    pair = 2
    for request in range(requests):
        length = lengths[request]
        blocks = STRETCH // home
        lo = request * blocks
        q_req = jnp.stack(
            [q_all[(lo + b) % 2, (lo + b) // 2]
             for b in range(blocks)], axis=0).astype(F32)
        q_req = q_req.reshape(blocks, KVH, home, width)
        key_pos = first_key + lax.broadcasted_iota(jnp.int32, (span, pair * STRETCH), 0)
        row_pos = length - STRETCH + lax.rem(
            lax.broadcasted_iota(jnp.int32, (span, pair * STRETCH), 1), STRETCH)
        allowed = key_pos <= row_pos
        for v in range(KVH):
            key_v = keys_ref[request, :, v * HD:(v + 1) * HD]
            val_v = values_ref[request, :, v * HD:(v + 1) * HD]
            val_t = val_v.astype(F32).T.astype(BF16)
            q_v = q_req[:, v].reshape(STRETCH, width)
            for g in range(0, GROUPS, pair):
                q_g = jnp.concatenate(
                    [q_v[:, (g + i) * HD:(g + i + 1) * HD] for i in range(pair)],
                    axis=0).astype(BF16)
                scores = dot(key_v, q_g, 1, 1) * HD ** (-0.5)
                scores = jnp.where(allowed, scores, -1e30)
                top = jnp.max(scores, axis=0, keepdims=True)
                weights = jnp.where(allowed, jnp.exp(scores - top), 0.0)
                total = jnp.sum(weights, axis=0, keepdims=True)
                mixed = dot(val_t, weights.astype(BF16), 1, 0).astype(BF16)
                for i in range(pair):
                    head = v * GROUPS + g + i
                    cols = slice(request * STRETCH, (request + 1) * STRETCH)
                    take = slice(i * STRETCH, (i + 1) * STRETCH)
                    for c in range(per_head):
                        j = head * per_head + c
                        mix_snd[j % 2, j // 2, :, cols] = mixed[c * chunk:(c + 1) * chunk, take]
                        st_snd[j % 2, 0, j // 2:j // 2 + 1, cols] = top[:, take]
                        st_snd[j % 2, 1, j // 2:j // 2 + 1, cols] = total[:, take]

    x_mix = remote(mix_snd.at[other], mix_rcv, pair_s.at[0], pair_r.at[0], sib)
    x_st = remote(st_snd.at[other], st_rcv, pair_s.at[1], pair_r.at[1], sib)
    x_st.start()
    x_mix.start()
    gather_forward(c_all, c_s, c_f, c_r)
    x_st.wait()
    x_mix.wait()
    top_a, top_b = st_snd[par, 0], st_rcv[0]
    best = jnp.maximum(top_a, top_b)
    fac_a, fac_b = jnp.exp(top_a - best), jnp.exp(top_b - best)
    total = st_snd[par, 1] * fac_a + st_rcv[1] * fac_b
    for q in range(half_n):
        s_snd[q, 0:1] = best[q:q + 1]
        s_snd[q, 1:2] = total[q:q + 1]
        m_snd[q] = (mix_snd[par, q].astype(F32) * fac_a[q:q + 1]
                    + mix_rcv[q].astype(F32) * fac_b[q:q + 1]).astype(BF16)

    def part_copies(k):
        p = peer(k)
        dev = p * 2 + par
        return (
            remote(s_snd.at[p], s_in.at[half], s_s.at[k], s_r.at[half], dev),
            remote(m_snd.at[p], m_in.at[half], m_s.at[k], m_r.at[half], dev),
        )

    def start_parts(k):
        for c in part_copies(k):
            c.start()

    each(1, half_n, start_parts)
    s_in[half, 0:2] = s_snd[half, 0:2]
    m_in[half] = m_snd[half]
    loads[0].wait()

    def wait_parts(k):
        p = peer(k)
        remote(s_snd.at[p], s_in.at[p], s_s.at[k], s_r.at[p], sib).wait_recv()
        remote(m_snd.at[p], m_in.at[p], m_s.at[k], m_r.at[p], sib).wait_recv()

    each(1, half_n, wait_parts)
    best = s_in[0, 0:1]
    for q in range(1, half_n):
        best = jnp.maximum(best, s_in[q, 0:1])
    denom = jnp.zeros_like(best)
    numer = jnp.zeros((chunk, rows), F32)
    for q in range(half_n):
        factor = jnp.exp(s_in[q, 0:1] - best)
        denom = denom + factor * s_in[q, 1:2]
        numer = numer + m_in[q].astype(F32) * factor
    attn = (numer / denom).astype(BF16)

    a_slots = dot(pick, attn, 1, 1).astype(BF16)
    a_snd[...] = a_slots.reshape(2, half_n, cap, chunk)

    def project(parity):
        part = dot(a_snd[parity].reshape(half_n * cap, chunk), ow[...], 1, 0)
        p_snd[parity] = part.astype(BF16).reshape(half_n, cap, D)

    project(other)
    x_p = remote(p_snd.at[other], p_rcv, pair_s.at[2], pair_r.at[2], sib)
    x_p.start()
    project(par)
    x_p.wait()

    def spread(mine, got, mid, into, ss, rs):
        def step(k):
            p = peer(k)
            mid[p] = (mine[par, p].astype(F32) + got[p].astype(F32)).astype(BF16)
            remote(mid.at[p], into.at[half], ss.at[k], rs.at[half], p * 2 + par).start()
        each(1, half_n, step)

    def collect(mine, got, mid, into, ss, rs):
        total = mine[par, half].astype(F32) + got[half].astype(F32)

        def step(k, total):
            p = lax.rem(half - k + half_n, half_n)
            remote(mid.at[p], into.at[p], ss.at[k], rs.at[p], sib).wait_recv()
            return total + into[p].astype(F32)
        return lax.fori_loop(1, half_n, step, total)

    spread(p_snd, p_rcv, p_mid, p_in, p_s, p_r)

    def attn_copy(k):
        to = lax.rem(me + k, n)
        return remote(a_snd.at[lax.rem(to, 2), to // 2], a_in.at[me],
                      a_s.at[k], a_r.at[me], to)

    each(1, n, lambda k: attn_copy(k).start())
    projected = collect(p_snd, p_rcv, p_mid, p_in, p_s, p_r)
    stream = (residual_ref[...].astype(F32) + projected).astype(BF16).astype(F32)
    normed = stream * lax.rsqrt(
        jnp.mean(stream * stream, axis=1, keepdims=True) + 1e-06) * gain_ref[...]
    n_all[par, half] = normed.astype(BF16)
    gather_start(n_all, n_s, n_r)
    gather_finish(c_all, c_s, c_f, c_r)
    loads[1].wait()
    loads[2].wait()
    gather_forward(n_all, n_s, n_f, n_r)
    gather_finish(n_all, n_s, n_f, n_r)

    lane = lax.broadcasted_iota(jnp.int32, (slots // 2, c_all.shape[-1]), 1)
    tile = 256

    def expert(parity):
        x = n_all[parity].reshape(slots // 2, D)

        def up(t, c):
            lo = pl.multiple_of(t * tile, tile)
            gate = dot(x, gu[:, pl.ds(lo, tile)], 1, 0)
            lift = dot(x, gu[:, pl.ds(EFF + lo, tile)], 1, 0)
            hid[:, pl.ds(lo, tile)] = (gate / (1.0 + jnp.exp(-gate)) * lift).astype(BF16)
            return c
        lax.fori_loop(0, EFF // tile, up, 0)
        routes = c_all[parity].reshape(slots // 2, c_all.shape[-1])
        weight = jnp.sum(jnp.where(lane == me, routes, 0.0), axis=1, keepdims=True)
        h = hid[...]

        def lower(t, c):
            lo = pl.multiple_of(t * tile, tile)
            part = dot(h, down[:, pl.ds(lo, tile)], 1, 0) * weight
            e_snd[parity, :, :, pl.ds(lo, tile)] = part.astype(BF16).reshape(
                half_n, cap, tile)
            return c
        lax.fori_loop(0, D // tile, lower, 0)

    expert(other)
    x_e = remote(e_snd.at[other], e_rcv, pair_s.at[3], pair_r.at[3], sib)
    x_e.start()
    expert(par)
    x_e.wait()
    spread(e_snd, e_rcv, e_mid, e_in, e_s, e_r)

    a_in[me] = a_snd[par, half]

    def wait_attn(k):
        at_k = lax.rem(me + k, n)
        remote(a_snd.at[0, 0], a_in.at[at_k], a_s.at[k], a_r.at[at_k], sib).wait_recv()

    each(1, n, wait_attn)
    attn_out[...] = jnp.concatenate([a_in[j] for j in range(n)], axis=1)

    moe = collect(e_snd, e_rcv, e_mid, e_in, e_s, e_r)
    layer_out[...] = jnp.where(own_valid, stream + moe, 0.0).astype(BF16)

    def drain(k):
        for c in part_copies(k):
            c.wait_send()
        remote(p_mid.at[0], p_in.at[0], p_s.at[k], p_r.at[0], sib).wait_send()
        remote(e_mid.at[0], e_in.at[0], e_s.at[k], e_r.at[0], sib).wait_send()

    each(1, half_n, drain)
    each(1, n, lambda k: attn_copy(k).wait_send())


def body(
    queries,
    keys,
    values,
    lengths,
    owner_counts,
    row_order,
    residual,
    out_weight,
    norm_gain,
    expert_ids,
    route_weights,
    gate_up,
    expert_down,
):
    n = lax.axis_size("ctx")
    half_n = n // 2
    home = queries.shape[0]
    rows = n * home
    cap = residual.shape[0]
    chunk = out_weight.shape[0]
    lanes = -(-n // LANES) * LANES
    vmem = pl.BlockSpec(memory_space=pltpu.VMEM)
    smem = pl.BlockSpec(memory_space=pltpu.SMEM)
    anywhere = pl.BlockSpec(memory_space=pl.ANY)
    dma = pltpu.SemaphoreType.DMA
    slot_block = (half_n, cap, D)
    scratch = [
        pltpu.VMEM(out_weight.shape, BF16),
        pltpu.VMEM(gate_up.shape[1:], BF16),
        pltpu.VMEM(expert_down.shape[1:], BF16),
        pltpu.VMEM((2, half_n, KVH * home, GROUPS * HD), BF16),
        pltpu.VMEM((2, half_n, cap, lanes), F32),
        pltpu.VMEM((2, half_n, chunk, rows), BF16),
        pltpu.VMEM((2, 2, half_n, rows), F32),
        pltpu.VMEM((half_n, chunk, rows), BF16),
        pltpu.VMEM((2, half_n, rows), F32),
        pltpu.VMEM((half_n, chunk, rows), BF16),
        pltpu.VMEM((half_n, 8, rows), F32),
        pltpu.VMEM((half_n, chunk, rows), BF16),
        pltpu.VMEM((half_n, 8, rows), F32),
        pltpu.VMEM((2, half_n, cap, chunk), BF16),
        pltpu.VMEM((n, cap, chunk), BF16),
        pltpu.VMEM((2,) + slot_block, BF16),
        pltpu.VMEM(slot_block, BF16),
        pltpu.VMEM(slot_block, BF16),
        pltpu.VMEM(slot_block, BF16),
        pltpu.VMEM((2,) + slot_block, BF16),
        pltpu.VMEM((half_n * cap, EFF), BF16),
        pltpu.VMEM((2,) + slot_block, BF16),
        pltpu.VMEM(slot_block, BF16),
        pltpu.VMEM(slot_block, BF16),
        pltpu.VMEM(slot_block, BF16),
        dma((3,)),
    ]
    gather = [dma((half_n,)), dma((half_n,)), dma((2, half_n))]
    exchange = [dma((half_n,)), dma((half_n,))]
    scratch += gather + gather
    scratch += [dma((4,)), dma((4,))]
    scratch += exchange + exchange
    scratch += [dma((n,)), dma((n,))]
    scratch += exchange + gather + exchange
    return pl.pallas_call(
        functools.partial(kernel, n),
        out_shape=(
            jax.ShapeDtypeStruct((cap, D), BF16),
            jax.ShapeDtypeStruct((cap, D), BF16),
        ),
        in_specs=[smem] + [vmem] * 9 + [anywhere] * 3,
        out_specs=(vmem, vmem),
        scratch_shapes=scratch,
        compiler_params=pltpu.CompilerParams(
            collective_id=0, has_side_effects=True, vmem_limit_bytes=60 * 2**20
        ),
    )(
        lengths,
        owner_counts.reshape(1, n),
        row_order.reshape(1, rows),
        queries,
        keys,
        values,
        residual,
        expert_ids,
        route_weights,
        norm_gain.reshape(1, D),
        out_weight,
        gate_up,
        expert_down,
    )


def solution(mesh):
    placed = (
        P(("groups", "ctx"), None),
        P("groups", "ctx", None),
        P("groups", "ctx", None),
        P("groups"),
        P("groups"),
        P("groups"),
        P(("groups", "ctx"), None),
        P("ctx", None),
        P(),
        P(("groups", "ctx"), None),
        P(("groups", "ctx"), None),
        P("ctx", None, None),
        P("ctx", None, None),
    )
    return jax.shard_map(
        body,
        mesh=mesh,
        in_specs=placed,
        out_specs=(P(("groups", "ctx"), None), P(("groups", "ctx"), None)),
        check_vma=False,
    )
```

time: 214 us -> 87.6 us (0.41)
  blocking collectives: 80.2 us -> 0 us
  Pallas kernels: 0 us -> 79.6 us
  waiting for transfers between devices: 53.6 us -> 0 us
  matrix products: 19.6 us -> 0 us
  starting transfers between devices: 18 us -> 0 us
  between operations: 15.3 us -> 1.29 us
  local copies, waits for them, and re-layouts: 18.6 us -> 5.66 us
  other arithmetic: 6.55 us -> 0 us
    pallas_call x0 -> x1, Pallas kernels: none -> 79.6 us  [body(): pl.pallas_call(functools.partial(kernel, n), out_shape=(jax.ShapeDtypeStr...]
    all_to_all x4 -> x0, waiting for transfers between devices: 52.9 us -> none  [the longest x1 25.6 us: body(): lax.all_to_all(mixed_home, 'ctx', split_axis=0, concat_axis=0, tiled=True)]
    all_gather x2 -> x0, blocking collectives: 52.7 us -> none  [the longest x1 27.6 us: body(): every_query = lax.all_gather(queries, 'ctx', axis=0, tiled=True)]
    all_to_all x1 -> x0, blocking collectives: 27.4 us -> none  [body(): lax.all_to_all(outgoing, 'ctx', split_axis=0, concat_axis=0, tiled=True)]
    dot_general x7 -> x0, matrix products: 19.6 us -> none  [the longest x1 4.69 us: body(): jnp.dot(attn_own, lax.all_gather(out_weight, 'ctx', axis=0, tiled=True),...]
    all_to_all x4 -> x0, starting transfers between devices: 17.9 us -> none  [the longest x1 6.02 us: body(): lax.all_to_all(mixed_home, 'ctx', split_axis=0, concat_axis=0, tiled=True)]
    gather x3 -> x0, local copies, waits for them, and re-layouts: 3.73 us -> none  [the longest x2 1.94 us: slot_table(): picked = row_order[jnp.clip(where_at, 0, total_rows - 1)]]
    reduce_sum x6 -> x0, other arithmetic: 2.96 us -> none  [the longest x1 1.56 us: merge_sources(): jnp.sum(mixed.reshape(sources, items, HQ, HD) * factor[..., None], axis=0)]
  transfers between devices with their start and end apart: 5 -> 0, of which waited for: 3 -> 0; matrix products, arithmetic and copies ran while one was open for 13% -> 0% of each run, Pallas kernels for 0% -> 0%
where the time goes in v1:
time: 87.6 us; the launch traced here: 86.5 us
  Pallas kernels  79.6 us (91%)
  local copies, waits for them, and re-layouts  5.66 us (6%)
  between operations  1.29 us (1%)
    pallas_call x1, Pallas kernels, body(): pl.pallas_call(functools.partial(kernel, n), out_shape=(jax.ShapeDtypeStr...  79.6 us
    unnamed x4, local copies, waits for them, and re-layouts  5.66 us

profile of v1, /device:TPU:0, one launch (start us, length us, event | category | flops | bytes accessed | tf_op | source)
XLA Modules:
  0.0 86.5 jit_solution(60962299365999864)
XLA Ops:
  1.3 1.4 %copy.15.ids_ref = s32[16,8]{1,0:T(8,128)} copy(s32[16,8]{0,1:T(8,128)} %param.22) | data formatting | bytes 1024 | tf_op args[9]
  2.6 1.4 %copy.16.route_ref = f32[16,8]{1,0:T(8,128)} copy(f32[16,8]{0,1:T(8,128)} %param.23) | data formatting | bytes 1024 | tf_op args[10]
  4.0 79.6 %shard_map.140 = (bf16[16,2048]{1,0:T(8,128)(2,1)}, bf16[16,2048]{1,0:T(8,128)(2,1)}) custom-call(s32[1]{0:T(128)S(6)} %copy.19.lengths, s32[1,16]{1,0:T(1,128)} %bitcast.4, s32[1,128]{1,0:T(1,128)} %bitcast.5, bf16[8,2048]{1,0:T(8,128)(2,1)} %q_ref.1, bf16[1,512,256]{2,1,0:T(8,128)(2,1)} %keys_ref.1, bf16[1,512,256]{2,1,0:T(8,128)(2,1)} %values_ref.1, ...), custom_call_target="tpu_custom_call" | custom-call | tf_op jit(solution)/shard_map/pallas_call | solution.py:461
  83.6 1.5 %copy.20 = bf16[16,2048]{1,0:T(8,128)(2,1)} copy(bf16[16,2048]{1,0:T(8,128)(2,1)} %get-tuple-element.4) | data formatting | bytes 131072
  85.0 1.5 %copy.21 = bf16[16,2048]{1,0:T(8,128)(2,1)} copy(bf16[16,2048]{1,0:T(8,128)(2,1)} %get-tuple-element.5) | data formatting | bytes 131072

commit v2 on v1

--- a/solution.py
+++ b/solution.py
@@ -61,17 +61,21 @@
     p_rcv,
     p_mid,
     p_in,
+    p_yin,
     n_all,
     hid,
     e_snd,
     e_rcv,
     e_mid,
     e_in,
+    e_yin,
     w_sem,
     q_s,
+    q_y,
     q_f,
     q_r,
     c_s,
+    c_y,
     c_f,
     c_r,
     pair_s,
@@ -83,12 +87,17 @@
     a_s,
     a_r,
     p_s,
+    p_y,
     p_r,
+    p_yr,
     n_s,
+    n_y,
     n_f,
     n_r,
     e_s,
+    e_y,
     e_r,
+    e_yr,
 ):
     half_n = n // 2
     home = q_ref.shape[0]
@@ -104,6 +113,10 @@
     other = 1 - par
     sib = half * 2 + other
 
+    ny = 2 if half_n % 2 == 0 else 1
+    nz = half_n // ny
+    z, y = half // ny, lax.rem(half, ny)
+
     def peer(k):
         return lax.rem(half + k, half_n)
 
@@ -145,8 +158,11 @@
     own_place = lax.broadcasted_iota(jnp.int32, (cap, 1), 0)
     _, own_valid = slot_info(cap, jnp.zeros((cap, 1), jnp.int32) + me, own_place)
 
-    ids = ids_ref[...]
-    route = route_ref[...]
+    def upright(flat):
+        return jnp.concatenate([flat, jnp.zeros((TOPK, LANES - cap), F32)], axis=1).T[:cap]
+
+    ids = upright(ids_ref[...].astype(F32)).astype(jnp.int32)
+    route = upright(route_ref[...])
     route = route / jnp.sum(route, axis=1, keepdims=True)
     expert_lane = lax.broadcasted_iota(jnp.int32, (cap, c_all.shape[-1]), 1)
     mixw = jnp.zeros((cap, c_all.shape[-1]), F32)
@@ -156,34 +172,62 @@
 
     pl.semaphore_wait(barrier, n - 1)
 
-    def gather_start(buf, ss, rs):
-        own = buf.at[par, half]
-        each(1, half_n, lambda k: remote(
-            own, own, ss.at[k], rs.at[par, half], peer(k) * 2 + par).start())
-        remote(own, own, ss.at[0], rs.at[par, half], sib).start()
-
-    def gather_forward(buf, ss, fs, rs):
+    def z_peer(k):
+        return lax.rem(z + k, nz) * ny + y
+
+    def y_peer(k):
+        return lax.rem(z + k, nz) * ny + (ny - 1 - y)
+
+    def block_copy(buf, pa, h, sem, rs, dev):
+        block = buf.at[pa, h]
+        return remote(block, block, sem, rs.at[pa, h], dev)
+
+    def gather_start(buf, sems):
+        ss, ys, fs, rs = sems
+        each(1, nz, lambda k: block_copy(
+            buf, par, half, ss.at[k], rs, z_peer(k) * 2 + par).start())
+        if ny > 1:
+            block_copy(buf, par, half, ys.at[0], rs, y_peer(0) * 2 + par).start()
+        block_copy(buf, par, half, ss.at[0], rs, sib).start()
+
+    def pass_on(buf, sems, h):
+        ss, ys, fs, rs = sems
+        block_copy(buf, par, h, ss.at[0], rs, sib).wait_recv()
+        block_copy(buf, par, h, fs.at[h], rs, sib).start()
+
+    def gather_z(buf, sems):
+        ss, ys, fs, rs = sems
+        if ny > 1:
+            pass_on(buf, sems, y_peer(0))
+
         def step(k):
-            q = lax.rem(half - k + half_n, half_n)
-            block = buf.at[par, q]
-            got = remote(block, block, ss.at[k], rs.at[par, q], sib)
-            got.wait_recv()
-            remote(block, block, fs.at[k], rs.at[par, q], sib).start()
-        each(1, half_n, step)
-
-    def gather_finish(buf, ss, fs, rs):
-        def step(q):
-            block = buf.at[other, q]
-            remote(block, block, ss.at[0], rs.at[other, q], sib).wait_recv()
-        each(0, half_n, step)
-        own = buf.at[par, half]
-        each(0, half_n, lambda k: remote(
-            own, own, ss.at[k], rs.at[par, half], sib).wait_send())
-        each(1, half_n, lambda k: remote(
-            own, own, fs.at[k], rs.at[par, half], sib).wait_send())
-
-    gather_start(q_all, q_s, q_r)
-    gather_start(c_all, c_s, c_r)
+            h = z_peer(nz - k)
+            pass_on(buf, sems, h)
+            if ny > 1:
+                block_copy(buf, par, h, ys.at[k], rs, y_peer(0) * 2 + par).start()
+        each(1, nz, step)
+
+    def gather_y(buf, sems):
+        if ny > 1:
+            each(1, nz, lambda k: pass_on(buf, sems, y_peer(nz - k)))
+
+    def gather_finish(buf, sems):
+        ss, ys, fs, rs = sems
+        each(0, half_n, lambda h: block_copy(
+            buf, other, h, ss.at[0], rs, sib).wait_recv())
+
+    def gather_drain(buf, sems):
+        ss, ys, fs, rs = sems
+        each(0, nz, lambda k: block_copy(buf, par, half, ss.at[k], rs, sib).wait_send())
+        if ny > 1:
+            each(0, nz, lambda k: block_copy(buf, par, half, ys.at[k], rs, sib).wait_send())
+        each(1, half_n, lambda k: block_copy(
+            buf, par, peer(k), fs.at[peer(k)], rs, sib).wait_send())
+
+    q_g = (q_s, q_y, q_f, q_r)
+    c_g = (c_s, c_y, c_f, c_r)
+    n_g = (n_s, n_y, n_f, n_r)
+    gather_start(q_all, q_g)
     for load in loads:
         load.start()
 
@@ -199,8 +243,10 @@
     row_of = jnp.where(filled, row_of, -1.0)
     pick = (row_lane == row_of).astype(BF16)
 
-    gather_forward(q_all, q_s, q_f, q_r)
-    gather_finish(q_all, q_s, q_f, q_r)
+    gather_z(q_all, q_g)
+    gather_y(q_all, q_g)
+    gather_finish(q_all, q_g)
+    gather_start(c_all, c_g)
 
     first_key = me * span
     per_head = HD // chunk
@@ -223,10 +269,10 @@
             val_t = val_v.astype(F32).T.astype(BF16)
             q_v = q_req[:, v].reshape(STRETCH, width)
             for g in range(0, GROUPS, pair):
-                q_g = jnp.concatenate(
+                q_pair = jnp.concatenate(
                     [q_v[:, (g + i) * HD:(g + i + 1) * HD] for i in range(pair)],
                     axis=0).astype(BF16)
-                scores = dot(key_v, q_g, 1, 1) * HD ** (-0.5)
+                scores = dot(key_v, q_pair, 1, 1) * HD ** (-0.5)
                 scores = jnp.where(allowed, scores, -1e30)
                 top = jnp.max(scores, axis=0, keepdims=True)
                 weights = jnp.where(allowed, jnp.exp(scores - top), 0.0)
@@ -246,7 +292,7 @@
     x_st = remote(st_snd.at[other], st_rcv, pair_s.at[1], pair_r.at[1], sib)
     x_st.start()
     x_mix.start()
-    gather_forward(c_all, c_s, c_f, c_r)
+    gather_z(c_all, c_g)
     x_st.wait()
     x_mix.wait()
     top_a, top_b = st_snd[par, 0], st_rcv[0]
@@ -272,6 +318,7 @@
             c.start()
 
     each(1, half_n, start_parts)
+    gather_y(c_all, c_g)
     s_in[half, 0:2] = s_snd[half, 0:2]
     m_in[half] = m_snd[half]
     loads[0].wait()
@@ -306,23 +353,49 @@
     project(par)
     x_p.wait()
 
-    def spread(mine, got, mid, into, ss, rs):
+    def spread(mine, got, mid, into, yin, ss, ys, rs, yr):
+        if ny > 1:
+            def step_y(k):
+                h = y_peer(k)
+                to = h // ny
+                mid[h] = (mine[par, h].astype(F32) + got[h].astype(F32)).astype(BF16)
+                remote(mid.at[h], yin.at[to], ys.at[k - 1], yr.at[to],
+                       y_peer(0) * 2 + par).start()
+            each(1, nz + 1, step_y)
+
         def step(k):
-            p = peer(k)
-            mid[p] = (mine[par, p].astype(F32) + got[p].astype(F32)).astype(BF16)
-            remote(mid.at[p], into.at[half], ss.at[k], rs.at[half], p * 2 + par).start()
-        each(1, half_n, step)
-
-    def collect(mine, got, mid, into, ss, rs):
+            h = z_peer(k)
+            total = mine[par, h].astype(F32) + got[h].astype(F32)
+            if ny > 1:
+                to = h // ny
+                remote(mid.at[h], yin.at[to], ss.at[k], yr.at[to], sib).wait_recv()
+                total = total + yin[to].astype(F32)
+            mid[h] = total.astype(BF16)
+            remote(mid.at[h], into.at[z], ss.at[k], rs.at[z], h * 2 + par).start()
+        each(1, nz, step)
+
+    def collect(mine, got, mid, into, yin, ss, ys, rs, yr):
         total = mine[par, half].astype(F32) + got[half].astype(F32)
+        if ny > 1:
+            remote(mid.at[0], yin.at[z], ss.at[0], yr.at[z], sib).wait_recv()
+            total = total + yin[z].astype(F32)
 
         def step(k, total):
-            p = lax.rem(half - k + half_n, half_n)
-            remote(mid.at[p], into.at[p], ss.at[k], rs.at[p], sib).wait_recv()
-            return total + into[p].astype(F32)
-        return lax.fori_loop(1, half_n, step, total)
-
-    spread(p_snd, p_rcv, p_mid, p_in, p_s, p_r)
+            at_z = lax.rem(z - k + nz, nz)
+            remote(mid.at[0], into.at[at_z], ss.at[k], rs.at[at_z], sib).wait_recv()
+            return total + into[at_z].astype(F32)
+        return lax.fori_loop(1, nz, step, total)
+
+    def drain_spread(mid, into, yin, ss, ys, rs, yr):
+        each(1, nz, lambda k: remote(
+            mid.at[0], into.at[0], ss.at[k], rs.at[0], sib).wait_send())
+        if ny > 1:
+            each(0, nz, lambda k: remote(
+                mid.at[0], yin.at[0], ys.at[k], yr.at[0], sib).wait_send())
+
+    p_x = (p_mid, p_in, p_yin, p_s, p_y, p_r, p_yr)
+    e_x = (e_mid, e_in, e_yin, e_s, e_y, e_r, e_yr)
+    spread(p_snd, p_rcv, *p_x)
 
     def attn_copy(k):
         to = lax.rem(me + k, n)
@@ -330,17 +403,18 @@
                       a_s.at[k], a_r.at[me], to)
 
     each(1, n, lambda k: attn_copy(k).start())
-    projected = collect(p_snd, p_rcv, p_mid, p_in, p_s, p_r)
+    projected = collect(p_snd, p_rcv, *p_x)
     stream = (residual_ref[...].astype(F32) + projected).astype(BF16).astype(F32)
     normed = stream * lax.rsqrt(
         jnp.mean(stream * stream, axis=1, keepdims=True) + 1e-06) * gain_ref[...]
     n_all[par, half] = normed.astype(BF16)
-    gather_start(n_all, n_s, n_r)
-    gather_finish(c_all, c_s, c_f, c_r)
+    gather_start(n_all, n_g)
+    gather_finish(c_all, c_g)
     loads[1].wait()
     loads[2].wait()
-    gather_forward(n_all, n_s, n_f, n_r)
-    gather_finish(n_all, n_s, n_f, n_r)
+    gather_z(n_all, n_g)
+    gather_y(n_all, n_g)
+    gather_finish(n_all, n_g)
 
     lane = lax.broadcasted_iota(jnp.int32, (slots // 2, c_all.shape[-1]), 1)
     tile = 256
@@ -372,7 +446,7 @@
     x_e.start()
     expert(par)
     x_e.wait()
-    spread(e_snd, e_rcv, e_mid, e_in, e_s, e_r)
+    spread(e_snd, e_rcv, *e_x)
 
     a_in[me] = a_snd[par, half]
 
@@ -383,16 +457,19 @@
     each(1, n, wait_attn)
     attn_out[...] = jnp.concatenate([a_in[j] for j in range(n)], axis=1)
 
-    moe = collect(e_snd, e_rcv, e_mid, e_in, e_s, e_r)
+    moe = collect(e_snd, e_rcv, *e_x)
     layer_out[...] = jnp.where(own_valid, stream + moe, 0.0).astype(BF16)
 
     def drain(k):
         for c in part_copies(k):
             c.wait_send()
-        remote(p_mid.at[0], p_in.at[0], p_s.at[k], p_r.at[0], sib).wait_send()
-        remote(e_mid.at[0], e_in.at[0], e_s.at[k], e_r.at[0], sib).wait_send()
 
     each(1, half_n, drain)
+    drain_spread(*p_x)
+    drain_spread(*e_x)
+    gather_drain(q_all, q_g)
+    gather_drain(c_all, c_g)
+    gather_drain(n_all, n_g)
     each(1, n, lambda k: attn_copy(k).wait_send())
 
 
@@ -423,6 +500,9 @@
     anywhere = pl.BlockSpec(memory_space=pl.ANY)
     dma = pltpu.SemaphoreType.DMA
     slot_block = (half_n, cap, D)
+    ny = 2 if half_n % 2 == 0 else 1
+    nz = half_n // ny
+    line_block = (nz, cap, D)
     scratch = [
         pltpu.VMEM(out_weight.shape, BF16),
         pltpu.VMEM(gate_up.shape[1:], BF16),
@@ -442,22 +522,25 @@
         pltpu.VMEM((2,) + slot_block, BF16),
         pltpu.VMEM(slot_block, BF16),
         pltpu.VMEM(slot_block, BF16),
-        pltpu.VMEM(slot_block, BF16),
+        pltpu.VMEM(line_block, BF16),
+        pltpu.VMEM(line_block, BF16),
         pltpu.VMEM((2,) + slot_block, BF16),
         pltpu.VMEM((half_n * cap, EFF), BF16),
         pltpu.VMEM((2,) + slot_block, BF16),
         pltpu.VMEM(slot_block, BF16),
         pltpu.VMEM(slot_block, BF16),
-        pltpu.VMEM(slot_block, BF16),
+        pltpu.VMEM(line_block, BF16),
+        pltpu.VMEM(line_block, BF16),
         dma((3,)),
     ]
-    gather = [dma((half_n,)), dma((half_n,)), dma((2, half_n))]
+    gather = [dma((nz,)), dma((nz,)), dma((half_n,)), dma((2, half_n))]
     exchange = [dma((half_n,)), dma((half_n,))]
+    staged = [dma((nz,)), dma((nz,)), dma((nz,)), dma((nz,))]
     scratch += gather + gather
     scratch += [dma((4,)), dma((4,))]
     scratch += exchange + exchange
     scratch += [dma((n,)), dma((n,))]
-    scratch += exchange + gather + exchange
+    scratch += staged + gather + staged
     return pl.pallas_call(
         functools.partial(kernel, n),
         out_shape=(
@@ -478,8 +561,8 @@
         keys,
         values,
         residual,
-        expert_ids,
-        route_weights,
+        expert_ids.T,
+        route_weights.T,
         norm_gain.reshape(1, D),
         out_weight,
         gate_up,

time: 87.6 us -> 79.5 us (0.908)
  Pallas kernels: 79.6 us -> 75 us
  local copies, waits for them, and re-layouts: 5.66 us -> 2.95 us
    pallas_call x1, Pallas kernels: 79.6 us -> 75 us  [body(): pl.pallas_call(functools.partial(kernel, n), out_shape=(jax.ShapeDtypeStr...]
    unnamed x4 -> x2, local copies, waits for them, and re-layouts: 5.66 us -> 2.95 us
where the time goes in v2:
time: 79.5 us; the launch traced here: 79.3 us
  Pallas kernels  75 us (94%)
  local copies, waits for them, and re-layouts  2.95 us (4%)
  between operations  1.29 us (2%)
    pallas_call x1, Pallas kernels, body(): pl.pallas_call(functools.partial(kernel, n), out_shape=(jax.ShapeDtypeStr...  75 us
    unnamed x2, local copies, waits for them, and re-layouts  2.95 us

profile of v2, /device:TPU:0, one launch (start us, length us, event | category | flops | bytes accessed | tf_op | source)
XLA Modules:
  0.0 79.3 jit_solution(3173737489220155139)
XLA Ops:
  1.3 75.0 %shard_map.140 = (bf16[16,2048]{1,0:T(8,128)(2,1)}, bf16[16,2048]{1,0:T(8,128)(2,1)}) custom-call(s32[1]{0:T(128)S(6)} %copy.17.lengths, s32[1,16]{1,0:T(1,128)} %bitcast.8, s32[1,128]{1,0:T(1,128)} %bitcast.9, bf16[8,2048]{1,0:T(8,128)(2,1)} %q_ref.1, bf16[1,512,256]{2,1,0:T(8,128)(2,1)} %keys_ref.1, bf16[1,512,256]{2,1,0:T(8,128)(2,1)} %values_ref.1, ...), custom_call_target="tpu_custom_call" | custom-call | tf_op jit(solution)/shard_map/pallas_call | solution.py:544
  76.3 1.5 %copy.18 = bf16[16,2048]{1,0:T(8,128)(2,1)} copy(bf16[16,2048]{1,0:T(8,128)(2,1)} %get-tuple-element.4) | data formatting | bytes 131072
  77.8 1.5 %copy.19 = bf16[16,2048]{1,0:T(8,128)(2,1)} copy(bf16[16,2048]{1,0:T(8,128)(2,1)} %get-tuple-element.5) | data formatting | bytes 131072

commit v3 on v2

--- a/solution.py
+++ b/solution.py
@@ -16,6 +16,7 @@
 STRETCH = 128
 GROUPS = HQ // KVH
 LANES = 128
+LOG2E = 1.4426950408889634
 F32 = jnp.float32
 BF16 = jnp.bfloat16
 MESH = pl.DeviceIdType.MESH
@@ -31,17 +32,19 @@
     counts_ref,
     order_ref,
     q_ref,
-    keys_ref,
-    values_ref,
-    residual_ref,
+    keys_hbm,
+    values_hbm,
+    residual_hbm,
     ids_ref,
     route_ref,
     gain_ref,
     ow_hbm,
     gu_hbm,
     down_hbm,
-    attn_out,
-    layer_out,
+    out,
+    keys_ref,
+    values_ref,
+    residual_ref,
     ow,
     gu,
     down,
@@ -136,7 +139,15 @@
         pltpu.make_async_copy(ow_hbm, ow, w_sem.at[0]),
         pltpu.make_async_copy(gu_hbm.at[0], gu, w_sem.at[1]),
         pltpu.make_async_copy(down_hbm.at[0], down, w_sem.at[2]),
+        pltpu.make_async_copy(residual_hbm, residual_ref, w_sem.at[5]),
     ]
+
+    cache = [
+        pltpu.make_async_copy(keys_hbm, keys_ref, w_sem.at[3]),
+        pltpu.make_async_copy(values_hbm, values_ref, w_sem.at[4]),
+    ]
+    for load in cache:
+        load.start()
 
     barrier = pltpu.get_barrier_semaphore()
     each(1, n, lambda k: pl.semaphore_signal(
@@ -247,6 +258,8 @@
     gather_y(q_all, q_g)
     gather_finish(q_all, q_g)
     gather_start(c_all, c_g)
+    for load in cache:
+        load.wait()
 
     first_key = me * span
     per_head = HD // chunk
@@ -272,12 +285,14 @@
                 q_pair = jnp.concatenate(
                     [q_v[:, (g + i) * HD:(g + i + 1) * HD] for i in range(pair)],
                     axis=0).astype(BF16)
-                scores = dot(key_v, q_pair, 1, 1) * HD ** (-0.5)
-                scores = jnp.where(allowed, scores, -1e30)
+                scores = jnp.where(allowed, dot(key_v, q_pair, 1, 1), -1e30)
                 top = jnp.max(scores, axis=0, keepdims=True)
-                weights = jnp.where(allowed, jnp.exp(scores - top), 0.0)
-                total = jnp.sum(weights, axis=0, keepdims=True)
-                mixed = dot(val_t, weights.astype(BF16), 1, 0).astype(BF16)
+                some = top > -1e29
+                weights = jnp.exp2((scores - top) * (HD ** (-0.5) * LOG2E))
+                total = jnp.where(some, jnp.sum(weights, axis=0, keepdims=True), 0.0)
+                mixed = dot(val_t, weights.astype(BF16), 1, 0)
+                mixed = jnp.where(some, mixed, 0.0).astype(BF16)
+                top = jnp.where(some, top * HD ** (-0.5), -1e30)
                 for i in range(pair):
                     head = v * GROUPS + g + i
                     cols = slice(request * STRETCH, (request + 1) * STRETCH)
@@ -322,6 +337,7 @@
     s_in[half, 0:2] = s_snd[half, 0:2]
     m_in[half] = m_snd[half]
     loads[0].wait()
+    loads[3].wait()
 
     def wait_parts(k):
         p = peer(k)
@@ -347,6 +363,12 @@
         part = dot(a_snd[parity].reshape(half_n * cap, chunk), ow[...], 1, 0)
         p_snd[parity] = part.astype(BF16).reshape(half_n, cap, D)
 
+    def attn_copy(k):
+        to = lax.rem(me + k, n)
+        return remote(a_snd.at[lax.rem(to, 2), to // 2], a_in.at[me],
+                      a_s.at[k], a_r.at[me], to)
+
+    each(1, n, lambda k: attn_copy(k).start())
     project(other)
     x_p = remote(p_snd.at[other], p_rcv, pair_s.at[2], pair_r.at[2], sib)
     x_p.start()
@@ -397,12 +419,6 @@
     e_x = (e_mid, e_in, e_yin, e_s, e_y, e_r, e_yr)
     spread(p_snd, p_rcv, *p_x)
 
-    def attn_copy(k):
-        to = lax.rem(me + k, n)
-        return remote(a_snd.at[lax.rem(to, 2), to // 2], a_in.at[me],
-                      a_s.at[k], a_r.at[me], to)
-
-    each(1, n, lambda k: attn_copy(k).start())
     projected = collect(p_snd, p_rcv, *p_x)
     stream = (residual_ref[...].astype(F32) + projected).astype(BF16).astype(F32)
     normed = stream * lax.rsqrt(
@@ -416,36 +432,37 @@
     gather_y(n_all, n_g)
     gather_finish(n_all, n_g)
 
-    lane = lax.broadcasted_iota(jnp.int32, (slots // 2, c_all.shape[-1]), 1)
+    lane = lax.broadcasted_iota(jnp.int32, (slots, c_all.shape[-1]), 1)
     tile = 256
-
-    def expert(parity):
-        x = n_all[parity].reshape(slots // 2, D)
-
-        def up(t, c):
-            lo = pl.multiple_of(t * tile, tile)
-            gate = dot(x, gu[:, pl.ds(lo, tile)], 1, 0)
-            lift = dot(x, gu[:, pl.ds(EFF + lo, tile)], 1, 0)
-            hid[:, pl.ds(lo, tile)] = (gate / (1.0 + jnp.exp(-gate)) * lift).astype(BF16)
-            return c
-        lax.fori_loop(0, EFF // tile, up, 0)
-        routes = c_all[parity].reshape(slots // 2, c_all.shape[-1])
-        weight = jnp.sum(jnp.where(lane == me, routes, 0.0), axis=1, keepdims=True)
-        h = hid[...]
-
-        def lower(t, c):
-            lo = pl.multiple_of(t * tile, tile)
-            part = dot(h, down[:, pl.ds(lo, tile)], 1, 0) * weight
-            e_snd[parity, :, :, pl.ds(lo, tile)] = part.astype(BF16).reshape(
-                half_n, cap, tile)
-            return c
-        lax.fori_loop(0, D // tile, lower, 0)
-
-    expert(other)
-    x_e = remote(e_snd.at[other], e_rcv, pair_s.at[3], pair_r.at[3], sib)
-    x_e.start()
-    expert(par)
-    x_e.wait()
+    x = n_all.reshape(slots, D)
+
+    def up(t, c):
+        lo = pl.multiple_of(t * tile, tile)
+        gate = dot(x[...], gu[:, pl.ds(lo, tile)], 1, 0)
+        lift = dot(x[...], gu[:, pl.ds(EFF + lo, tile)], 1, 0)
+        hid[:, pl.ds(lo, tile)] = (gate / (1.0 + jnp.exp(-gate)) * lift).astype(BF16)
+        return c
+    lax.fori_loop(0, EFF // tile, up, 0)
+    routes = c_all[...].reshape(slots, c_all.shape[-1])
+    weight = jnp.sum(jnp.where(lane == me, routes, 0.0), axis=1, keepdims=True)
+
+    def lower(t, c):
+        lo = pl.multiple_of(t * tile, tile)
+        part = dot(hid[...], down[:, pl.ds(lo, tile)], 1, 0) * weight
+        e_snd[:, :, :, pl.ds(lo, tile)] = part.astype(BF16).reshape(2, half_n, cap, tile)
+        return c
+
+    sides = []
+    side = D // 2
+    for i in range(2):
+        lax.fori_loop(i * side // tile, (i + 1) * side // tile, lower, 0)
+        cols = pl.ds(i * side, side)
+        sides.append(remote(
+            e_snd.at[other, :, :, cols], e_rcv.at[:, :, cols],
+            pair_s.at[3 + i], pair_r.at[3 + i], sib))
+        sides[i].start()
+    for x_e in sides:
+        x_e.wait()
     spread(e_snd, e_rcv, *e_x)
 
     a_in[me] = a_snd[par, half]
@@ -455,10 +472,10 @@
         remote(a_snd.at[0, 0], a_in.at[at_k], a_s.at[k], a_r.at[at_k], sib).wait_recv()
 
     each(1, n, wait_attn)
-    attn_out[...] = jnp.concatenate([a_in[j] for j in range(n)], axis=1)
+    out[0] = jnp.concatenate([a_in[j] for j in range(n)], axis=1)
 
     moe = collect(e_snd, e_rcv, *e_x)
-    layer_out[...] = jnp.where(own_valid, stream + moe, 0.0).astype(BF16)
+    out[1] = jnp.where(own_valid, stream + moe, 0.0).astype(BF16)
 
     def drain(k):
         for c in part_copies(k):
@@ -504,6 +521,9 @@
     nz = half_n // ny
     line_block = (nz, cap, D)
     scratch = [
+        pltpu.VMEM(keys.shape, BF16),
+        pltpu.VMEM(values.shape, BF16),
+        pltpu.VMEM(residual.shape, BF16),
         pltpu.VMEM(out_weight.shape, BF16),
         pltpu.VMEM(gate_up.shape[1:], BF16),
         pltpu.VMEM(expert_down.shape[1:], BF16),
@@ -525,30 +545,27 @@
         pltpu.VMEM(line_block, BF16),
         pltpu.VMEM(line_block, BF16),
         pltpu.VMEM((2,) + slot_block, BF16),
-        pltpu.VMEM((half_n * cap, EFF), BF16),
+        pltpu.VMEM((n * cap, EFF), BF16),
         pltpu.VMEM((2,) + slot_block, BF16),
         pltpu.VMEM(slot_block, BF16),
         pltpu.VMEM(slot_block, BF16),
         pltpu.VMEM(line_block, BF16),
         pltpu.VMEM(line_block, BF16),
-        dma((3,)),
+        dma((6,)),
     ]
     gather = [dma((nz,)), dma((nz,)), dma((half_n,)), dma((2, half_n))]
     exchange = [dma((half_n,)), dma((half_n,))]
     staged = [dma((nz,)), dma((nz,)), dma((nz,)), dma((nz,))]
     scratch += gather + gather
-    scratch += [dma((4,)), dma((4,))]
+    scratch += [dma((5,)), dma((5,))]
     scratch += exchange + exchange
     scratch += [dma((n,)), dma((n,))]
     scratch += staged + gather + staged
-    return pl.pallas_call(
+    out = pl.pallas_call(
         functools.partial(kernel, n),
-        out_shape=(
-            jax.ShapeDtypeStruct((cap, D), BF16),
-            jax.ShapeDtypeStruct((cap, D), BF16),
-        ),
-        in_specs=[smem] + [vmem] * 9 + [anywhere] * 3,
-        out_specs=(vmem, vmem),
+        out_shape=jax.ShapeDtypeStruct((2, cap, D), BF16),
+        in_specs=[smem] + [vmem] * 3 + [anywhere] * 3 + [vmem] * 3 + [anywhere] * 3,
+        out_specs=vmem,
         scratch_shapes=scratch,
         compiler_params=pltpu.CompilerParams(
             collective_id=0, has_side_effects=True, vmem_limit_bytes=60 * 2**20
@@ -568,6 +585,7 @@
         gate_up,
         expert_down,
     )
+    return out[0], out[1]
 
 
 def solution(mesh):

time: 79.5 us -> 78.6 us (0.989)
  local copies, waits for them, and re-layouts: 2.95 us -> 1.53 us
    unnamed x2 -> x0, local copies, waits for them, and re-layouts: 2.95 us -> none
    squeeze x0 -> x1, local copies, waits for them, and re-layouts: none -> 1.53 us  [body(): return (out[0], out[1])]
where the time goes in v3:
time: 78.6 us; the launch traced here: 78.3 us
  Pallas kernels  75.5 us (96%)
  local copies, waits for them, and re-layouts  1.53 us (2%)
  between operations  1.29 us (2%)
    pallas_call x1, Pallas kernels, body(): pl.pallas_call(functools.partial(kernel, n), out_shape=jax.ShapeDtypeStru...  75.5 us

profile of v3, /device:TPU:0, one launch (start us, length us, event | category | flops | bytes accessed | tf_op | source)
XLA Modules:
  0.0 78.3 jit_solution(4097418865531332160)
XLA Ops:
  1.3 75.5 %shard_map.140 = bf16[2,16,2048]{2,1,0:T(8,128)(2,1)} custom-call(s32[1]{0:T(128)S(6)} %copy.15.lengths, s32[1,16]{1,0:T(1,128)} %bitcast.12, s32[1,128]{1,0:T(1,128)} %bitcast.13, bf16[8,2048]{1,0:T(8,128)(2,1)} %q_ref.1, bf16[1,512,256]{2,1,0:T(8,128)(2,1)} %keys_hbm.1, bf16[1,512,256]{2,1,0:T(8,128)(2,1)} %values_hbm.1, bf16[16,2048]{1,0:T(8,128)(2,1)} %residual_hbm.1, ...), custom_call_target="tpu_custom_call" | custom-call | tf_op jit(solution)/shard_map/pallas_call | solution.py:564
  76.8 1.5 %slice_bitcast_fusion = (bf16[16,2048]{1,0:T(8,128)(2,1)}, bf16[16,2048]{1,0:T(8,128)(2,1)}) fusion(bf16[2,16,2048]{2,1,0:T(8,128)(2,1)} %shard_map.140), kind=kLoop, calls=%fused_computation | loop fusion | bytes 262144 | tf_op jit(solution)/shard_map/squeeze | solution.py:588

commit v4 on v3

--- a/solution.py
+++ b/solution.py
@@ -44,7 +44,6 @@
     out,
     keys_ref,
     values_ref,
-    residual_ref,
     ow,
     gu,
     down,
@@ -65,7 +64,10 @@
     p_mid,
     p_in,
     p_yin,
+    r_all,
     n_all,
+    x_buf,
+    str_buf,
     hid,
     e_snd,
     e_rcv,
@@ -93,6 +95,10 @@
     p_y,
     p_r,
     p_yr,
+    r_s,
+    r_y,
+    r_f,
+    r_r,
     n_s,
     n_y,
     n_f,
@@ -105,7 +111,7 @@
     half_n = n // 2
     home = q_ref.shape[0]
     rows = n * home
-    cap = residual_ref.shape[0]
+    cap = residual_hbm.shape[0]
     slots = n * cap
     chunk = ow.shape[0]
     span = keys_ref.shape[1]
@@ -139,13 +145,14 @@
         pltpu.make_async_copy(ow_hbm, ow, w_sem.at[0]),
         pltpu.make_async_copy(gu_hbm.at[0], gu, w_sem.at[1]),
         pltpu.make_async_copy(down_hbm.at[0], down, w_sem.at[2]),
-        pltpu.make_async_copy(residual_hbm, residual_ref, w_sem.at[5]),
     ]
 
     cache = [
         pltpu.make_async_copy(keys_hbm, keys_ref, w_sem.at[3]),
         pltpu.make_async_copy(values_hbm, values_ref, w_sem.at[4]),
     ]
+    load_res = pltpu.make_async_copy(residual_hbm, r_all.at[par, half], w_sem.at[5])
+    load_res.start()
     for load in cache:
         load.start()
 
@@ -237,6 +244,7 @@
 
     q_g = (q_s, q_y, q_f, q_r)
     c_g = (c_s, c_y, c_f, c_r)
+    r_g = (r_s, r_y, r_f, r_r)
     n_g = (n_s, n_y, n_f, n_r)
     gather_start(q_all, q_g)
     for load in loads:
@@ -253,11 +261,20 @@
     row_of = jnp.sum(jnp.where(row_lane == at, order, 0.0), axis=1, keepdims=True)
     row_of = jnp.where(filled, row_of, -1.0)
     pick = (row_lane == row_of).astype(BF16)
+    lane = lax.broadcasted_iota(jnp.int32, (slots, rows), 1)
+    block_lane = lane // home
+    device_lane = lax.rem(block_lane, half_n) * 2 + block_lane // half_n
+    row_lane = (device_lane * home + lax.rem(lane, home)).astype(F32)
+    pick_par = (row_lane == row_of).astype(BF16)
+    own_lane = me * home + lax.broadcasted_iota(jnp.int32, (slots, LANES), 1)
+    pick_own = (own_lane.astype(F32) == row_of).astype(BF16)
 
     gather_z(q_all, q_g)
     gather_y(q_all, q_g)
     gather_finish(q_all, q_g)
     gather_start(c_all, c_g)
+    load_res.wait()
+    gather_start(r_all, r_g)
     for load in cache:
         load.wait()
 
@@ -334,10 +351,10 @@
 
     each(1, half_n, start_parts)
     gather_y(c_all, c_g)
+    gather_z(r_all, r_g)
     s_in[half, 0:2] = s_snd[half, 0:2]
     m_in[half] = m_snd[half]
     loads[0].wait()
-    loads[3].wait()
 
     def wait_parts(k):
         p = peer(k)
@@ -359,20 +376,21 @@
     a_slots = dot(pick, attn, 1, 1).astype(BF16)
     a_snd[...] = a_slots.reshape(2, half_n, cap, chunk)
 
-    def project(parity):
-        part = dot(a_snd[parity].reshape(half_n * cap, chunk), ow[...], 1, 0)
-        p_snd[parity] = part.astype(BF16).reshape(half_n, cap, D)
-
     def attn_copy(k):
         to = lax.rem(me + k, n)
         return remote(a_snd.at[lax.rem(to, 2), to // 2], a_in.at[me],
                       a_s.at[k], a_r.at[me], to)
 
     each(1, n, lambda k: attn_copy(k).start())
-    project(other)
+    part = dot(attn, ow[...], 0, 0)
+    wide = D // 2
+    for d in range(n):
+        own = part[d * home:(d + 1) * home]
+        p_snd[d % 2, d // 2] = jnp.concatenate(
+            [own[:, :wide], own[:, wide:]], axis=0).astype(BF16)
     x_p = remote(p_snd.at[other], p_rcv, pair_s.at[2], pair_r.at[2], sib)
     x_p.start()
-    project(par)
+    gather_y(r_all, r_g)
     x_p.wait()
 
     def spread(mine, got, mid, into, yin, ss, ys, rs, yr):
@@ -419,12 +437,23 @@
     e_x = (e_mid, e_in, e_yin, e_s, e_y, e_r, e_yr)
     spread(p_snd, p_rcv, *p_x)
 
+    gather_finish(r_all, r_g)
+    held = dot(pick_own, r_all[...].reshape(slots, D), 0, 0)[:home]
+    held = jnp.concatenate([held[:, :wide], held[:, wide:]], axis=0)
     projected = collect(p_snd, p_rcv, *p_x)
-    stream = (residual_ref[...].astype(F32) + projected).astype(BF16).astype(F32)
-    normed = stream * lax.rsqrt(
-        jnp.mean(stream * stream, axis=1, keepdims=True) + 1e-06) * gain_ref[...]
+    stream = (held + projected).astype(BF16).astype(F32)
+    square = jnp.sum(stream * stream, axis=1, keepdims=True)
+    scale = lax.rsqrt((square[:home] + square[home:]) / D + 1e-06)
+    gain = gain_ref[...]
+    gain = jnp.concatenate(
+        [jnp.broadcast_to(gain[:, :wide], (home, wide)),
+         jnp.broadcast_to(gain[:, wide:], (home, wide))], axis=0)
+    normed = stream * jnp.concatenate([scale, scale], axis=0) * gain
     n_all[par, half] = normed.astype(BF16)
     gather_start(n_all, n_g)
+    blank = jnp.zeros((LANES - home, D), F32)
+    str_buf[...] = jnp.concatenate(
+        [jnp.concatenate([stream[:home], stream[home:]], axis=1), blank], axis=0).astype(BF16)
     gather_finish(c_all, c_g)
     loads[1].wait()
     loads[2].wait()
@@ -434,12 +463,14 @@
 
     lane = lax.broadcasted_iota(jnp.int32, (slots, c_all.shape[-1]), 1)
     tile = 256
-    x = n_all.reshape(slots, D)
+    halves = n_all[...].astype(F32).reshape(n, 2, home, wide)
+    x_buf[:, :wide] = halves[:, 0].reshape(rows, wide).astype(BF16)
+    x_buf[:, wide:] = halves[:, 1].reshape(rows, wide).astype(BF16)
 
     def up(t, c):
         lo = pl.multiple_of(t * tile, tile)
-        gate = dot(x[...], gu[:, pl.ds(lo, tile)], 1, 0)
-        lift = dot(x[...], gu[:, pl.ds(EFF + lo, tile)], 1, 0)
+        gate = dot(x_buf[...], gu[:, pl.ds(lo, tile)], 1, 0)
+        lift = dot(x_buf[...], gu[:, pl.ds(EFF + lo, tile)], 1, 0)
         hid[:, pl.ds(lo, tile)] = (gate / (1.0 + jnp.exp(-gate)) * lift).astype(BF16)
         return c
     lax.fori_loop(0, EFF // tile, up, 0)
@@ -448,7 +479,9 @@
 
     def lower(t, c):
         lo = pl.multiple_of(t * tile, tile)
-        part = dot(hid[...], down[:, pl.ds(lo, tile)], 1, 0) * weight
+        result = dot(hid[...], down[:, pl.ds(lo, tile)], 1, 0).astype(BF16)
+        part = dot(pick_par, result, 1, 0) * weight
+        part = part + dot(pick_own, str_buf[:, pl.ds(lo, tile)], 1, 0)
         e_snd[:, :, :, pl.ds(lo, tile)] = part.astype(BF16).reshape(2, half_n, cap, tile)
         return c
 
@@ -475,7 +508,7 @@
     out[0] = jnp.concatenate([a_in[j] for j in range(n)], axis=1)
 
     moe = collect(e_snd, e_rcv, *e_x)
-    out[1] = jnp.where(own_valid, stream + moe, 0.0).astype(BF16)
+    out[1] = jnp.where(own_valid, moe, 0.0).astype(BF16)
 
     def drain(k):
         for c in part_copies(k):
@@ -486,6 +519,7 @@
     drain_spread(*e_x)
     gather_drain(q_all, q_g)
     gather_drain(c_all, c_g)
+    gather_drain(r_all, r_g)
     gather_drain(n_all, n_g)
     each(1, n, lambda k: attn_copy(k).wait_send())
 
@@ -520,10 +554,10 @@
     ny = 2 if half_n % 2 == 0 else 1
     nz = half_n // ny
     line_block = (nz, cap, D)
+    row_block = (half_n, 2 * home, D // 2)
     scratch = [
         pltpu.VMEM(keys.shape, BF16),
         pltpu.VMEM(values.shape, BF16),
-        pltpu.VMEM(residual.shape, BF16),
         pltpu.VMEM(out_weight.shape, BF16),
         pltpu.VMEM(gate_up.shape[1:], BF16),
         pltpu.VMEM(expert_down.shape[1:], BF16),
@@ -539,13 +573,16 @@
         pltpu.VMEM((half_n, 8, rows), F32),
         pltpu.VMEM((2, half_n, cap, chunk), BF16),
         pltpu.VMEM((n, cap, chunk), BF16),
+        pltpu.VMEM((2,) + row_block, BF16),
+        pltpu.VMEM(row_block, BF16),
+        pltpu.VMEM(row_block, BF16),
+        pltpu.VMEM((nz,) + row_block[1:], BF16),
+        pltpu.VMEM((nz,) + row_block[1:], BF16),
         pltpu.VMEM((2,) + slot_block, BF16),
-        pltpu.VMEM(slot_block, BF16),
-        pltpu.VMEM(slot_block, BF16),
-        pltpu.VMEM(line_block, BF16),
-        pltpu.VMEM(line_block, BF16),
-        pltpu.VMEM((2,) + slot_block, BF16),
-        pltpu.VMEM((n * cap, EFF), BF16),
+        pltpu.VMEM((2,) + row_block, BF16),
+        pltpu.VMEM((rows, D), BF16),
+        pltpu.VMEM((LANES, D), BF16),
+        pltpu.VMEM((rows, EFF), BF16),
         pltpu.VMEM((2,) + slot_block, BF16),
         pltpu.VMEM(slot_block, BF16),
         pltpu.VMEM(slot_block, BF16),
@@ -560,7 +597,7 @@
     scratch += [dma((5,)), dma((5,))]
     scratch += exchange + exchange
     scratch += [dma((n,)), dma((n,))]
-    scratch += staged + gather + staged
+    scratch += staged + gather + gather + staged
     out = pl.pallas_call(
         functools.partial(kernel, n),
         out_shape=jax.ShapeDtypeStruct((2, cap, D), BF16),

time: 78.6 us -> 72 us (0.916)
  Pallas kernels: 75.5 us -> 68.9 us
    pallas_call x1, Pallas kernels: 75.5 us -> 68.9 us  [body(): pl.pallas_call(functools.partial(kernel, n), out_shape=jax.ShapeDtypeStru...]
where the time goes in v4:
time: 72 us; the launch traced here: 71.7 us
  Pallas kernels  68.9 us (96%)
  local copies, waits for them, and re-layouts  1.53 us (2%)
  between operations  1.29 us (2%)
    pallas_call x1, Pallas kernels, body(): pl.pallas_call(functools.partial(kernel, n), out_shape=jax.ShapeDtypeStru...  68.9 us
    squeeze x1, local copies, waits for them, and re-layouts, body(): return (out[0], out[1])  1.53 us

profile of v4, /device:TPU:0, one launch (start us, length us, event | category | flops | bytes accessed | tf_op | source)
XLA Modules:
  0.0 71.7 jit_solution(10479774368183217655)
XLA Ops:
  1.3 68.9 %shard_map.140 = bf16[2,16,2048]{2,1,0:T(8,128)(2,1)} custom-call(s32[1]{0:T(128)S(6)} %copy.15.lengths, s32[1,16]{1,0:T(1,128)} %bitcast.12, s32[1,128]{1,0:T(1,128)} %bitcast.13, bf16[8,2048]{1,0:T(8,128)(2,1)} %q_ref.1, bf16[1,512,256]{2,1,0:T(8,128)(2,1)} %keys_hbm.1, bf16[1,512,256]{2,1,0:T(8,128)(2,1)} %values_hbm.1, bf16[16,2048]{1,0:T(8,128)(2,1)} %residual_hbm.1, ...), custom_call_target="tpu_custom_call" | custom-call | tf_op jit(solution)/shard_map/pallas_call | solution.py:601
  70.2 1.5 %slice_bitcast_fusion = (bf16[16,2048]{1,0:T(8,128)(2,1)}, bf16[16,2048]{1,0:T(8,128)(2,1)}) fusion(bf16[2,16,2048]{2,1,0:T(8,128)(2,1)} %shard_map.140), kind=kLoop, calls=%fused_computation | loop fusion | bytes 262144 | tf_op jit(solution)/shard_map/squeeze | solution.py:625

commit v5 on v4

--- a/solution.py
+++ b/solution.py
@@ -282,7 +282,7 @@
     per_head = HD // chunk
     pair = 2
     for request in range(requests):
-        length = lengths[request]
+        length = lengths[:, request:request + 1]
         blocks = STRETCH // home
         lo = request * blocks
         q_req = jnp.stack(
@@ -381,7 +381,6 @@
         return remote(a_snd.at[lax.rem(to, 2), to // 2], a_in.at[me],
                       a_s.at[k], a_r.at[me], to)
 
-    each(1, n, lambda k: attn_copy(k).start())
     part = dot(attn, ow[...], 0, 0)
     wide = D // 2
     for d in range(n):
@@ -393,7 +392,7 @@
     gather_y(r_all, r_g)
     x_p.wait()
 
-    def spread(mine, got, mid, into, yin, ss, ys, rs, yr):
+    def spread_y(mine, got, mid, into, yin, ss, ys, rs, yr):
         if ny > 1:
             def step_y(k):
                 h = y_peer(k)
@@ -403,6 +402,7 @@
                        y_peer(0) * 2 + par).start()
             each(1, nz + 1, step_y)
 
+    def spread_z(mine, got, mid, into, yin, ss, ys, rs, yr):
         def step(k):
             h = z_peer(k)
             total = mine[par, h].astype(F32) + got[h].astype(F32)
@@ -434,8 +434,10 @@
                 mid.at[0], yin.at[0], ys.at[k], yr.at[0], sib).wait_send())
 
     p_x = (p_mid, p_in, p_yin, p_s, p_y, p_r, p_yr)
-    e_x = (e_mid, e_in, e_yin, e_s, e_y, e_r, e_yr)
-    spread(p_snd, p_rcv, *p_x)
+    e_x = [[ref.at[i] for ref in (
+        e_snd, e_rcv, e_mid, e_in, e_yin, e_s, e_y, e_r, e_yr)] for i in range(2)]
+    spread_y(p_snd, p_rcv, *p_x)
+    spread_z(p_snd, p_rcv, *p_x)
 
     gather_finish(r_all, r_g)
     held = dot(pick_own, r_all[...].reshape(slots, D), 0, 0)[:home]
@@ -459,44 +461,60 @@
     loads[2].wait()
     gather_z(n_all, n_g)
     gather_y(n_all, n_g)
+
+    def repack(parity):
+        halves = n_all[parity].astype(F32).reshape(half_n, 2, home, wide)
+        x_buf[parity, :, :wide] = halves[:, 0].reshape(rows // 2, wide).astype(BF16)
+        x_buf[parity, :, wide:] = halves[:, 1].reshape(rows // 2, wide).astype(BF16)
+
+    repack(par)
     gather_finish(n_all, n_g)
+    repack(other)
 
     lane = lax.broadcasted_iota(jnp.int32, (slots, c_all.shape[-1]), 1)
     tile = 256
-    halves = n_all[...].astype(F32).reshape(n, 2, home, wide)
-    x_buf[:, :wide] = halves[:, 0].reshape(rows, wide).astype(BF16)
-    x_buf[:, wide:] = halves[:, 1].reshape(rows, wide).astype(BF16)
+    each(1, n, lambda k: attn_copy(k).start())
+
+    x = x_buf.reshape(rows, D)
 
     def up(t, c):
         lo = pl.multiple_of(t * tile, tile)
-        gate = dot(x_buf[...], gu[:, pl.ds(lo, tile)], 1, 0)
-        lift = dot(x_buf[...], gu[:, pl.ds(EFF + lo, tile)], 1, 0)
+        gate = dot(x[...], gu[:, pl.ds(lo, tile)], 1, 0)
+        lift = dot(x[...], gu[:, pl.ds(EFF + lo, tile)], 1, 0)
         hid[:, pl.ds(lo, tile)] = (gate / (1.0 + jnp.exp(-gate)) * lift).astype(BF16)
         return c
     lax.fori_loop(0, EFF // tile, up, 0)
     routes = c_all[...].reshape(slots, c_all.shape[-1])
     weight = jnp.sum(jnp.where(lane == me, routes, 0.0), axis=1, keepdims=True)
 
-    def lower(t, c):
-        lo = pl.multiple_of(t * tile, tile)
-        result = dot(hid[...], down[:, pl.ds(lo, tile)], 1, 0).astype(BF16)
-        part = dot(pick_par, result, 1, 0) * weight
-        part = part + dot(pick_own, str_buf[:, pl.ds(lo, tile)], 1, 0)
-        e_snd[:, :, :, pl.ds(lo, tile)] = part.astype(BF16).reshape(2, half_n, cap, tile)
-        return c
-
-    sides = []
     side = D // 2
-    for i in range(2):
-        lax.fori_loop(i * side // tile, (i + 1) * side // tile, lower, 0)
-        cols = pl.ds(i * side, side)
-        sides.append(remote(
-            e_snd.at[other, :, :, cols], e_rcv.at[:, :, cols],
-            pair_s.at[3 + i], pair_r.at[3 + i], sib))
-        sides[i].start()
-    for x_e in sides:
-        x_e.wait()
-    spread(e_snd, e_rcv, *e_x)
+
+    def lower(i, first, last):
+        def step(t, c):
+            lo = pl.multiple_of(t * tile, tile)
+            cols = pl.ds(pl.multiple_of(i * side + lo, tile), tile)
+            result = dot(hid[...], down[:, cols], 1, 0).astype(BF16)
+            part = dot(pick_par, result, 1, 0) * weight
+            part = part + dot(pick_own, str_buf[:, cols], 1, 0)
+            e_snd[i, :, :, :, pl.ds(lo, tile)] = part.astype(BF16).reshape(
+                2, half_n, cap, tile)
+            return c
+        lax.fori_loop(first, last, step, 0)
+
+    x_e = [remote(e_snd.at[i, other], e_rcv.at[i], pair_s.at[3 + i], pair_r.at[3 + i], sib)
+           for i in range(2)]
+    tiles = side // tile
+    lower(0, 0, tiles)
+    x_e[0].start()
+    lower(1, 0, tiles // 2)
+    x_e[0].wait()
+    spread_y(*e_x[0])
+    lower(1, tiles // 2, tiles)
+    x_e[1].start()
+    spread_z(*e_x[0])
+    x_e[1].wait()
+    spread_y(*e_x[1])
+    spread_z(*e_x[1])
 
     a_in[me] = a_snd[par, half]
 
@@ -507,7 +525,7 @@
     each(1, n, wait_attn)
     out[0] = jnp.concatenate([a_in[j] for j in range(n)], axis=1)
 
-    moe = collect(e_snd, e_rcv, *e_x)
+    moe = jnp.concatenate([collect(*e_x[i]) for i in range(2)], axis=1)
     out[1] = jnp.where(own_valid, moe, 0.0).astype(BF16)
 
     def drain(k):
@@ -516,7 +534,8 @@
 
     each(1, half_n, drain)
     drain_spread(*p_x)
-    drain_spread(*e_x)
+    drain_spread(*e_x[0][2:])
+    drain_spread(*e_x[1][2:])
     gather_drain(q_all, q_g)
     gather_drain(c_all, c_g)
     gather_drain(r_all, r_g)
@@ -547,13 +566,12 @@
     chunk = out_weight.shape[0]
     lanes = -(-n // LANES) * LANES
     vmem = pl.BlockSpec(memory_space=pltpu.VMEM)
-    smem = pl.BlockSpec(memory_space=pltpu.SMEM)
     anywhere = pl.BlockSpec(memory_space=pl.ANY)
     dma = pltpu.SemaphoreType.DMA
     slot_block = (half_n, cap, D)
     ny = 2 if half_n % 2 == 0 else 1
     nz = half_n // ny
-    line_block = (nz, cap, D)
+    side_block = (half_n, cap, D // 2)
     row_block = (half_n, 2 * home, D // 2)
     scratch = [
         pltpu.VMEM(keys.shape, BF16),
@@ -580,14 +598,14 @@
         pltpu.VMEM((nz,) + row_block[1:], BF16),
         pltpu.VMEM((2,) + slot_block, BF16),
         pltpu.VMEM((2,) + row_block, BF16),
-        pltpu.VMEM((rows, D), BF16),
+        pltpu.VMEM((2, rows // 2, D), BF16),
         pltpu.VMEM((LANES, D), BF16),
         pltpu.VMEM((rows, EFF), BF16),
-        pltpu.VMEM((2,) + slot_block, BF16),
-        pltpu.VMEM(slot_block, BF16),
-        pltpu.VMEM(slot_block, BF16),
-        pltpu.VMEM(line_block, BF16),
-        pltpu.VMEM(line_block, BF16),
+        pltpu.VMEM((2, 2) + side_block, BF16),
+        pltpu.VMEM((2,) + side_block, BF16),
+        pltpu.VMEM((2,) + side_block, BF16),
+        pltpu.VMEM((2, nz) + side_block[1:], BF16),
+        pltpu.VMEM((2, nz) + side_block[1:], BF16),
         dma((6,)),
     ]
     gather = [dma((nz,)), dma((nz,)), dma((half_n,)), dma((2, half_n))]
@@ -597,18 +615,18 @@
     scratch += [dma((5,)), dma((5,))]
     scratch += exchange + exchange
     scratch += [dma((n,)), dma((n,))]
-    scratch += staged + gather + gather + staged
+    scratch += staged + gather + gather + [dma((2, nz))] * 4
     out = pl.pallas_call(
         functools.partial(kernel, n),
         out_shape=jax.ShapeDtypeStruct((2, cap, D), BF16),
-        in_specs=[smem] + [vmem] * 3 + [anywhere] * 3 + [vmem] * 3 + [anywhere] * 3,
+        in_specs=[vmem] * 4 + [anywhere] * 3 + [vmem] * 3 + [anywhere] * 3,
         out_specs=vmem,
         scratch_shapes=scratch,
         compiler_params=pltpu.CompilerParams(
             collective_id=0, has_side_effects=True, vmem_limit_bytes=60 * 2**20
         ),
     )(
-        lengths,
+        lengths.reshape(1, keys.shape[0]),
         owner_counts.reshape(1, n),
         row_order.reshape(1, rows),
         queries,

time: 72 us -> 70.3 us (0.976)
  Pallas kernels: 68.9 us -> 67.3 us
    pallas_call x1, Pallas kernels: 68.9 us -> 67.3 us  [body(): pl.pallas_call(functools.partial(kernel, n), out_shape=jax.ShapeDtypeStru...]
where the time goes in v5:
time: 70.3 us; the launch traced here: 70.1 us
  Pallas kernels  67.3 us (96%)
  local copies, waits for them, and re-layouts  1.53 us (2%)
  between operations  1.29 us (2%)
    pallas_call x1, Pallas kernels, body(): pl.pallas_call(functools.partial(kernel, n), out_shape=jax.ShapeDtypeStru...  67.3 us
    squeeze x1, local copies, waits for them, and re-layouts, body(): return (out[0], out[1])  1.53 us

profile of v5, /device:TPU:0, one launch (start us, length us, event | category | flops | bytes accessed | tf_op | source)
XLA Modules:
  0.0 70.1 jit_solution(14955339168677190263)
XLA Ops:
  1.3 67.3 %shard_map.140 = bf16[2,16,2048]{2,1,0:T(8,128)(2,1)} custom-call(s32[1,1]{1,0:T(1,128)} %bitcast.10.lengths, s32[1,16]{1,0:T(1,128)} %bitcast.14, s32[1,128]{1,0:T(1,128)} %bitcast.15, bf16[8,2048]{1,0:T(8,128)(2,1)} %q_ref.1, bf16[1,512,256]{2,1,0:T(8,128)(2,1)} %keys_hbm.1, bf16[1,512,256]{2,1,0:T(8,128)(2,1)} %values_hbm.1, ...), custom_call_target="tpu_custom_call" | custom-call | tf_op jit(solution)/shard_map/pallas_call | solution.py:619
  68.5 1.5 %slice_bitcast_fusion = (bf16[16,2048]{1,0:T(8,128)(2,1)}, bf16[16,2048]{1,0:T(8,128)(2,1)}) fusion(bf16[2,16,2048]{2,1,0:T(8,128)(2,1)} %shard_map.140), kind=kLoop, calls=%fused_computation | loop fusion | bytes 262144 | tf_op jit(solution)/shard_map/squeeze | solution.py:643

commit v6 on v5

--- a/solution.py
+++ b/solution.py
@@ -190,11 +190,23 @@
 
     pl.semaphore_wait(barrier, n - 1)
 
+    def z_to(k):
+        k = lax.rem(k, nz)
+        if nz & (nz - 1):
+            return lax.rem(z + k, nz)
+        to, bit = 0, 1
+        while bit < nz:
+            to = to + lax.rem(z // bit + k // bit, 2) * bit
+            bit = bit * 2
+        return to
+
     def z_peer(k):
-        return lax.rem(z + k, nz) * ny + y
+        return z_to(k) * ny + y
 
     def y_peer(k):
-        return lax.rem(z + k, nz) * ny + (ny - 1 - y)
+        return z_to(k) * ny + (ny - 1 - y)
+
+    z_own_y = z * ny + (ny - 1 - y)
 
     def block_copy(buf, pa, h, sem, rs, dev):
         block = buf.at[pa, h]
@@ -205,7 +217,7 @@
         each(1, nz, lambda k: block_copy(
             buf, par, half, ss.at[k], rs, z_peer(k) * 2 + par).start())
         if ny > 1:
-            block_copy(buf, par, half, ys.at[0], rs, y_peer(0) * 2 + par).start()
+            block_copy(buf, par, half, ys.at[0], rs, z_own_y * 2 + par).start()
         block_copy(buf, par, half, ss.at[0], rs, sib).start()
 
     def pass_on(buf, sems, h):
@@ -216,18 +228,18 @@
     def gather_z(buf, sems):
         ss, ys, fs, rs = sems
         if ny > 1:
-            pass_on(buf, sems, y_peer(0))
+            pass_on(buf, sems, z_own_y)
 
         def step(k):
-            h = z_peer(nz - k)
+            h = z_peer(k)
             pass_on(buf, sems, h)
             if ny > 1:
-                block_copy(buf, par, h, ys.at[k], rs, y_peer(0) * 2 + par).start()
+                block_copy(buf, par, h, ys.at[k], rs, z_own_y * 2 + par).start()
         each(1, nz, step)
 
     def gather_y(buf, sems):
         if ny > 1:
-            each(1, nz, lambda k: pass_on(buf, sems, y_peer(nz - k)))
+            each(1, nz, lambda k: pass_on(buf, sems, y_peer(k)))
 
     def gather_finish(buf, sems):
         ss, ys, fs, rs = sems
@@ -395,16 +407,16 @@
     def spread_y(mine, got, mid, into, yin, ss, ys, rs, yr):
         if ny > 1:
             def step_y(k):
-                h = y_peer(k)
+                h = y_peer(nz - k)
                 to = h // ny
                 mid[h] = (mine[par, h].astype(F32) + got[h].astype(F32)).astype(BF16)
                 remote(mid.at[h], yin.at[to], ys.at[k - 1], yr.at[to],
-                       y_peer(0) * 2 + par).start()
+                       z_own_y * 2 + par).start()
             each(1, nz + 1, step_y)
 
     def spread_z(mine, got, mid, into, yin, ss, ys, rs, yr):
         def step(k):
-            h = z_peer(k)
+            h = z_peer(nz - k)
             total = mine[par, h].astype(F32) + got[h].astype(F32)
             if ny > 1:
                 to = h // ny
@@ -511,9 +523,9 @@
     spread_y(*e_x[0])
     lower(1, tiles // 2, tiles)
     x_e[1].start()
-    spread_z(*e_x[0])
     x_e[1].wait()
     spread_y(*e_x[1])
+    spread_z(*e_x[0])
     spread_z(*e_x[1])
 
     a_in[me] = a_snd[par, half]

time: 70.3 us -> 69.4 us (0.987)
  Pallas kernels: 67.3 us -> 66.4 us
    pallas_call x1, Pallas kernels: 67.3 us -> 66.4 us  [body(): pl.pallas_call(functools.partial(kernel, n), out_shape=jax.ShapeDtypeStru...]
where the time goes in v6:
time: 69.4 us; the launch traced here: 69.2 us
  Pallas kernels  66.4 us (96%)
  local copies, waits for them, and re-layouts  1.53 us (2%)
  between operations  1.29 us (2%)
    pallas_call x1, Pallas kernels, body(): pl.pallas_call(functools.partial(kernel, n), out_shape=jax.ShapeDtypeStru...  66.4 us
    squeeze x1, local copies, waits for them, and re-layouts, body(): return (out[0], out[1])  1.53 us

profile of v6, /device:TPU:0, one launch (start us, length us, event | category | flops | bytes accessed | tf_op | source)
XLA Modules:
  0.0 69.2 jit_solution(6897795235190935053)
XLA Ops:
  1.3 66.4 %shard_map.140 = bf16[2,16,2048]{2,1,0:T(8,128)(2,1)} custom-call(s32[1,1]{1,0:T(1,128)} %bitcast.10.lengths, s32[1,16]{1,0:T(1,128)} %bitcast.14, s32[1,128]{1,0:T(1,128)} %bitcast.15, bf16[8,2048]{1,0:T(8,128)(2,1)} %q_ref.1, bf16[1,512,256]{2,1,0:T(8,128)(2,1)} %keys_hbm.1, bf16[1,512,256]{2,1,0:T(8,128)(2,1)} %values_hbm.1, ...), custom_call_target="tpu_custom_call" | custom-call | tf_op jit(solution)/shard_map/pallas_call | solution.py:631
  67.7 1.5 %slice_bitcast_fusion = (bf16[16,2048]{1,0:T(8,128)(2,1)}, bf16[16,2048]{1,0:T(8,128)(2,1)}) fusion(bf16[2,16,2048]{2,1,0:T(8,128)(2,1)} %shard_map.140), kind=kLoop, calls=%fused_computation | loop fusion | bytes 262144 | tf_op jit(solution)/shard_map/squeeze | solution.py:655

commit v7 on v6

--- a/solution.py
+++ b/solution.py
@@ -363,7 +363,6 @@
 
     each(1, half_n, start_parts)
     gather_y(c_all, c_g)
-    gather_z(r_all, r_g)
     s_in[half, 0:2] = s_snd[half, 0:2]
     m_in[half] = m_snd[half]
     loads[0].wait()
@@ -374,6 +373,7 @@
         remote(m_snd.at[p], m_in.at[p], m_s.at[k], m_r.at[p], sib).wait_recv()
 
     each(1, half_n, wait_parts)
+    gather_z(r_all, r_g)
     best = s_in[0, 0:1]
     for q in range(1, half_n):
         best = jnp.maximum(best, s_in[q, 0:1])

time: 69.4 us -> 74.2 us (1.069)
  Pallas kernels: 66.4 us -> 71.1 us
    pallas_call x1, Pallas kernels: 66.4 us -> 71.1 us  [body(): pl.pallas_call(functools.partial(kernel, n), out_shape=jax.ShapeDtypeStru...]
where the time goes in v7:
time: 74.2 us; the launch traced here: 74 us
  Pallas kernels  71.1 us (96%)
  local copies, waits for them, and re-layouts  1.53 us (2%)
  between operations  1.29 us (2%)
    pallas_call x1, Pallas kernels, body(): pl.pallas_call(functools.partial(kernel, n), out_shape=jax.ShapeDtypeStru...  71.1 us
    squeeze x1, local copies, waits for them, and re-layouts, body(): return (out[0], out[1])  1.53 us

profile of v7, /device:TPU:0, one launch (start us, length us, event | category | flops | bytes accessed | tf_op | source)
XLA Modules:
  0.0 74.0 jit_solution(8084391166566407662)
XLA Ops:
  1.3 71.1 %shard_map.140 = bf16[2,16,2048]{2,1,0:T(8,128)(2,1)} custom-call(s32[1,1]{1,0:T(1,128)} %bitcast.10.lengths, s32[1,16]{1,0:T(1,128)} %bitcast.14, s32[1,128]{1,0:T(1,128)} %bitcast.15, bf16[8,2048]{1,0:T(8,128)(2,1)} %q_ref.1, bf16[1,512,256]{2,1,0:T(8,128)(2,1)} %keys_hbm.1, bf16[1,512,256]{2,1,0:T(8,128)(2,1)} %values_hbm.1, ...), custom_call_target="tpu_custom_call" | custom-call | tf_op jit(solution)/shard_map/pallas_call | solution.py:631
  72.4 1.5 %slice_bitcast_fusion = (bf16[16,2048]{1,0:T(8,128)(2,1)}, bf16[16,2048]{1,0:T(8,128)(2,1)}) fusion(bf16[2,16,2048]{2,1,0:T(8,128)(2,1)} %shard_map.140), kind=kLoop, calls=%fused_computation | loop fusion | bytes 262144 | tf_op jit(solution)/shard_map/squeeze | solution.py:655
